TPU v7x, 32 devices: a whole 2x2x4 slice. The times are simulated.
32 devices in a mesh: seq: 4 (over y, core), exp: 8 (over z, x).
Axes of the slice: x: 2, y: 2, z: 4, core: 2. Of those that a mesh axis runs over, the one named last changes fastest.
Arguments:
- x_act: bfloat16 [8, 512, 4096], P('exp', 'seq'), may hold values from -6 to 6
- dt_low: bfloat16 [8, 512, 256], P('exp', 'seq'), may hold values from -6 to 6
- b_c: float32 [8, 512, 32], P('exp', 'seq'), may hold values from -6 to 6
- w_dt: bfloat16 [256, 4096], replicated, may hold values from -0.375 to 0.375
- dt_bias: float32 [4096], replicated, may hold values from -6 to -1
- a_log: float32 [16, 4096], replicated, may hold values from -1 to 2
- d_skip: float32 [4096], replicated, may hold values from 0.5 to 1.5
- w_router: bfloat16 [4, 4096], replicated, may hold values from -0.09375 to 0.09375
- expert_ids: int32 [8, 512, 2], P('exp', 'seq'), may hold values from 0 to 3, all different within a row; in each aligned block of 128 rows (0 to 127, 128 to 255, ..., all dimensions but the last counted through in order) at most 80 rows name the same one
- w_up: bfloat16 [8, 4096, 640], P('exp', 'seq'), may hold values from -0.09375 to 0.09375
- w_down: bfloat16 [8, 640, 4096], P('exp', None, 'seq'), may hold values from -0.15625 to 0.15625
Outputs:
- layer_out: bfloat16 [8, 512, 4096], P('exp', 'seq')
Inputs may be any that keep to these rules, and one draw needn't show every extreme that they name: `expert_ids`: within the 128 tokens of one device (an aligned block), no expert is chosen by more than 80 tokens, and in some blocks one expert is chosen by exactly 80; a token's two experts differ.
All inputs are finite; a program needn't handle non-finite values.
Results may differ from a plain program's by a relative error of at most 0.011.
Values may be sent and summed in bfloat16 or wider, within the bound.
A program may use at most 128 MiB of HBM per device.

v0:
```python
import jax
import jax.numpy as jnp
from jax import lax
from jax.sharding import PartitionSpec as P


def from_behind(value, axis, by):
    count = lax.axis_size(axis)
    pairs = [(i, i + by) for i in range(count) if 0 <= i + by < count]
    return lax.ppermute(value, axis, pairs)


def carry_in(decay_total, end_state):

    def relay(index, incoming):
        return from_behind(decay_total * incoming + end_state, "seq", 1)

    return lax.fori_loop(0, lax.axis_size("seq") - 1, relay, jnp.zeros_like(end_state))


def sweep(start_state, a_neg, delta, driven, b_in, c_out):
    tokens_here, channels = delta.shape
    nstate = b_in.shape[1]
    group = 8
    turns = tokens_here // group

    def advance(state, inputs):
        rate, drive, b_rows, c_rows = inputs
        results = []
        for inner in range(group):
            state = (
                jnp.exp(a_neg * rate[inner][None, :]) * state
                + drive[inner][None, :] * b_rows[inner][:, None]
            )
            results.append(jnp.sum(c_rows[inner][:, None] * state, axis=0))
        return (state, jnp.stack(results))

    inputs = (
        delta.reshape(turns, group, channels),
        driven.reshape(turns, group, channels),
        b_in.reshape(turns, group, nstate),
        c_out.reshape(turns, group, nstate),
    )
    final, results = lax.scan(advance, start_state, inputs)
    return (final, results.reshape(tokens_here, channels))


def per_device(
    x_act, dt_low, b_c, w_dt, dt_bias, a_log, d_skip, w_router, expert_ids, w_up, w_down
):
    tokens_here = x_act.shape[1]
    channels = x_act.shape[2]
    nstate = a_log.shape[0]
    xfloat = x_act[0].astype(jnp.float32)
    pre = jnp.dot(dt_low[0], w_dt, preferred_element_type=jnp.float32)
    delta = jax.nn.softplus(pre + dt_bias)
    a_neg = -jnp.exp(a_log)
    driven = delta * xfloat
    b_in = b_c[0, :, :nstate]
    c_out = b_c[0, :, nstate:]
    cumulated = jnp.cumsum(delta, axis=0)
    decay_total = jnp.exp(a_neg * cumulated[-1][None, :])
    pieces = max(1, channels // 512)
    span = channels // pieces
    ends = []
    for lower in range(0, channels, span):
        exponent = a_neg[None, :, lower : lower + span] * (
            cumulated[-1, lower : lower + span][None, None, :]
            - cumulated[:, None, lower : lower + span]
        )
        ends.append(
            jnp.sum(
                jnp.exp(exponent) * driven[:, None, lower : lower + span] * b_in[:, :, None], axis=0
            )
        )
    start = carry_in(decay_total, jnp.concatenate(ends, axis=1))
    _, scanned = sweep(start, a_neg, delta, driven, b_in, c_out)
    mixer = (scanned + d_skip * xfloat).astype(jnp.bfloat16)
    experts_count = w_router.shape[0]
    owners = lax.axis_size("exp")
    capacity = 5 * tokens_here // owners
    picks = expert_ids[0]
    logits = jnp.dot(mixer, w_router.T, preferred_element_type=jnp.float32)
    chosen = jnp.take_along_axis(logits, picks, axis=1)
    first = jax.nn.sigmoid(chosen[:, 0] - chosen[:, 1])
    second = 1.0 - first
    flat_ids = picks.reshape(-1)
    onehot = (flat_ids[:, None] == jnp.arange(experts_count, dtype=jnp.int32)[None, :]).astype(
        jnp.int32
    )
    position = jnp.sum(onehot * jnp.cumsum(onehot, axis=0), axis=1) - 1
    token_index = jnp.arange(2 * tokens_here, dtype=jnp.int32) // 2
    buffer = (
        jnp.zeros((experts_count, capacity, channels), jnp.bfloat16)
        .at[flat_ids, position]
        .set(mixer[token_index])
    )
    outgoing = jnp.repeat(buffer, 2, axis=0)
    incoming = lax.all_to_all(outgoing, "exp", split_axis=0, concat_axis=0, tiled=True)
    rows = incoming.reshape(-1, channels)
    pre_hidden = jnp.dot(
        rows, lax.all_gather(w_up, "seq", axis=1, tiled=True)[0], preferred_element_type=jnp.float32
    )
    hidden = jax.nn.silu(pre_hidden).astype(jnp.bfloat16)
    partial_out = lax.optimization_barrier(
        jnp.dot(
            hidden,
            lax.all_gather(w_down, "seq", axis=2, tiled=True)[0],
            preferred_element_type=jnp.float32,
        ).astype(jnp.bfloat16)
    )
    partial_out = partial_out.reshape(owners, capacity, channels)
    returned = lax.all_to_all(partial_out, "exp", split_axis=0, concat_axis=0, tiled=True)
    paired = returned.reshape(experts_count, 2, capacity, channels)
    combined = (paired[:, 0].astype(jnp.float32) + paired[:, 1].astype(jnp.float32)).astype(
        jnp.bfloat16
    )
    picked = combined[flat_ids, position].reshape(tokens_here, 2, channels).astype(jnp.float32)
    routed = first[:, None] * picked[:, 0] + second[:, None] * picked[:, 1]
    return (mixer.astype(jnp.float32) + routed).astype(jnp.bfloat16)[None]


def solution(mesh):
    in_specs = (
        P("exp", "seq", None),
        P("exp", "seq", None),
        P("exp", "seq", None),
        P(),
        P(),
        P(),
        P(),
        P(),
        P("exp", "seq", None),
        P("exp", "seq", None),
        P("exp", None, "seq"),
    )
    out_specs = P("exp", "seq", None)
    return jax.shard_map(
        per_device, mesh=mesh, in_specs=in_specs, out_specs=out_specs, check_vma=False
    )
```

profile of v0, /device:TPU:0, one launch (start us, length us, event | category | flops | bytes accessed | tf_op | source)
XLA Modules:
  0.0 511.3 jit_solution(736550182289984780)
XLA Ops:
  6.5 0.7 all-gather.3.cloned.1.call-update
  7.3 0.9 copy-done
  8.1 4.8 fusion.4
  12.9 3.5 reduce_window_sum.26
  16.4 0.7 fusion.31
  17.8 0.7 fusion.33
  18.5 2.7 fusion.32
  21.3 2.8 slice_subtract_fusion.2
  24.1 2.6 multiply_reduce_fusion.9
  26.9 6.6 %multiply_reduce_fusion.8 = (f32[16,512]{1,0:T(8,128)S(1)}, f32[16,512]{1,0:T(8,128)S(1)}, f32[16,512]{1,0:T(8,128)S(1)}, f32[16,512]{1,0:T(8,128)S(1)}, f32[16,512]{1,0:T(8,128)S(1)}, /*index=5*/f32[16,512]{1,0:T(8,128)S(1)}) fusion(f32[128,512]{1,0:T(8,128)S(1)} %get-tuple-element.178, f32[128,512]{1,0:T(8,128)S(1)} %get-tuple-element.162, ...), kind=kLoop, calls=%fused_computation.63 | loop fusion | flops 25116672 | bytes 3547136 | tf_op jit(solution)/shard_map/reduce_sum | solution.py:72
  33.6 24.7 %while.22 = (s32[]{:T(128)}, f32[16,4096]{1,0:T(8,128)S(1)}, f32[16,4096]{1,0:T(8,128)S(1)}, f32[16,4096]{1,0:T(8,128)S(1)}, s32[]{:T(128)}) while((s32[]{:T(128)}, f32[16,4096]{1,0:T(8,128)S(1)}, f32[16,4096]{1,0:T(8,128)S(1)}, f32[16,4096]{1,0:T(8,128)S(1)}, s32[]{:T(128)}) %tuple.131), condition=%wide.region_10.11_spmd, body=%wide.region_9.10_spmd.sunk | while | flops 131074 | bytes 2097253 | solution.py:18
  33.7 2.3 collective-permute-start
  36.1 1.1 collective-permute-done
  37.2 12.2 %collective-permute-start = (f32[16,4096]{1,0:T(8,128)S(1)}, f32[16,4096]{1,0:T(8,128)S(1)}, u32[]{:S(2)}, u32[]{:S(2)}) collective-permute-start(f32[16,4096]{1,0:T(8,128)S(1)} %multiply_add_fusion.12), channel_id=1, source_target_pairs={{0,8},{8,16},{16,24},{1,9},{9,17},{17,25},{2,10},{10,18},{18,26},{... | collective-permute-start | bytes 786440 | tf_op jit(solution)/shard_map/while/body/eval_jaxpr/ppermute | solution.py:10
  49.4 1.1 collective-permute-done
  50.6 6.6 %collective-permute-start = (f32[16,4096]{1,0:T(8,128)S(1)}, f32[16,4096]{1,0:T(8,128)S(1)}, u32[]{:S(2)}, u32[]{:S(2)}) collective-permute-start(f32[16,4096]{1,0:T(8,128)S(1)} %multiply_add_fusion.12), channel_id=1, source_target_pairs={{0,8},{8,16},{16,24},{1,9},{9,17},{17,25},{2,10},{10,18},{18,26},{... | collective-permute-start | bytes 786440 | tf_op jit(solution)/shard_map/while/body/eval_jaxpr/ppermute | solution.py:10
  57.2 1.1 collective-permute-done
  58.3 73.1 %while.23 = (s32[]{:T(128)}, f32[16,4096]{1,0:T(8,128)S(1)}, f32[16,8,4096]{2,1,0:T(8,128)}, f32[16,8,4096]{2,1,0:T(8,128)}, f32[16,4096]{1,0:T(8,128)S(1)}, /*i...) while((s32[]{:T(128)}, f32[16,4096]{1,0:T(8,128)S(1)}, ...), condition=%wide.region_20.21_spmd, body=%wide.region_11.20_spmd.sunk | while | flops 4685833 | bytes 3741845 | solution.py:44
  58.3 2.6 constant_dynamic-slice_fusion.21
  63.1 2.3 constant_dynamic-slice_fusion.21
  67.6 2.3 constant_dynamic-slice_fusion.21
  71.3 0.7 bitcast_dynamic-update-slice_fusion.2
  72.0 2.5 constant_dynamic-slice_fusion.21
  76.0 0.7 bitcast_dynamic-update-slice_fusion.2
  76.7 2.1 constant_dynamic-slice_fusion.21
  80.3 0.7 bitcast_dynamic-update-slice_fusion.2
  81.0 2.6 constant_dynamic-slice_fusion.21
  85.1 0.7 bitcast_dynamic-update-slice_fusion.2
  85.7 2.3 constant_dynamic-slice_fusion.21
  89.5 0.7 bitcast_dynamic-update-slice_fusion.2
  90.2 2.4 constant_dynamic-slice_fusion.21
  94.1 0.7 bitcast_dynamic-update-slice_fusion.2
  94.7 2.0 constant_dynamic-slice_fusion.21
  98.9 2.3 constant_dynamic-slice_fusion.21
  102.7 0.7 bitcast_dynamic-update-slice_fusion.2
  103.4 2.3 constant_dynamic-slice_fusion.21
  107.2 0.7 bitcast_dynamic-update-slice_fusion.2
  107.8 2.6 constant_dynamic-slice_fusion.21
  112.0 0.7 bitcast_dynamic-update-slice_fusion.2
  112.6 2.5 constant_dynamic-slice_fusion.21
  116.7 0.7 bitcast_dynamic-update-slice_fusion.2
  117.4 2.6 constant_dynamic-slice_fusion.21
  121.4 0.7 bitcast_dynamic-update-slice_fusion.2
  122.1 2.6 constant_dynamic-slice_fusion.21
  126.9 2.4 constant_dynamic-slice_fusion.21
  130.8 0.7 bitcast_dynamic-update-slice_fusion.2
  132.0 1.2 reduce-window.6
  133.6 1.9 fusion.7
  135.4 3.2 gather_fusion
  138.8 1.8 broadcast_in_dim.17
  140.6 66.9 %scatter_fusion = bf16[4,80,4096]{2,1,0:T(8,128)(2,1)} fusion(bf16[4,80,4096]{2,1,0:T(8,128)(2,1)} %broadcast_in_dim.17, s32[256]{0:T(256)S(1)} %bitcast.221, bf16[256,4096]{1,0:T(8,128)(2,1)} %gather_fusion), kind=kCustom, calls=%fused_computation.3 | custom fusion | bytes 6293504 | tf_op jit(solution)/shard_map/scatter | solution.py:96
  207.5 4.6 broadcast_in_dim.18
  212.2 5.9 %all-to-all-start = ((bf16[8,80,4096]{2,1,0:T(8,128)(2,1)}), bf16[8,80,4096]{2,1,0:T(8,128)(2,1)}, u32[]{:S(2)}, u32[]{:S(2)}) async-start(bf16[8,80,4096]{2,1,0:T(8,128)(2,1)} %bitcast.219), calls=%async_computation | async-start | bytes 10485760 | tf_op jit(solution)/shard_map/all_to_all | solution.py:99
  218.8 113.3 %all-to-all-done = bf16[8,80,4096]{2,1,0:T(8,128)(2,1)} async-done(((bf16[8,80,4096]{2,1,0:T(8,128)(2,1)}), bf16[8,80,4096]{2,1,0:T(8,128)(2,1)}, u32[]{:S(2)}, u32[]{:S(2)}) %all-to-all-start) | async-done | bytes 5242912 | tf_op jit(solution)/shard_map/all_to_all | solution.py:99
  332.1 8.4 %multiply_convert_fusion = bf16[640,640]{1,0:T(8,128)(2,1)S(1)} fusion(bf16[640,4096]{1,0:T(8,128)(2,1)} %bitcast.68, bf16[1,4096,640]{2,1,0:T(8,128)(2,1)} %all-gather.3.cloned.1.call-done), kind=kOutput, calls=%fused_computation.89 | convolution fusion | flops 3357491200 | bytes 11304960 | tf_op jit(solution)/shard_map/dot_general | solution.py:101
  340.5 8.5 %convolution_convert_fusion = bf16[640,4096]{1,0:T(8,128)(2,1)} fusion(bf16[640,640]{1,0:T(8,128)(2,1)S(1)} %multiply_convert_fusion, bf16[1,640,4096]{2,1,0:T(8,128)(2,1)} %all-gather.5.cloned.1.call-done), kind=kOutput, calls=%fused_computation.56 | convolution fusion | flops 3358064640 | bytes 11304960 | tf_op jit(solution)/shard_map/dot_general | solution.py:106
  349.0 6.8 %all-to-all-start.1 = ((bf16[8,80,4096]{2,1,0:T(8,128)(2,1)}), bf16[8,80,4096]{2,1,0:T(8,128)(2,1)}, u32[]{:S(2)}, u32[]{:S(2)}) async-start(bf16[8,80,4096]{2,1,0:T(8,128)(2,1)} %bitcast.222), calls=%async_computation.1 | async-start | bytes 10485760 | tf_op jit(solution)/shard_map/all_to_all | solution.py:113
  356.4 2.4 gather_fusion.2
  359.1 114.1 %all-to-all-done.1 = bf16[8,80,4096]{2,1,0:T(8,128)(2,1)} async-done(((bf16[8,80,4096]{2,1,0:T(8,128)(2,1)}), bf16[8,80,4096]{2,1,0:T(8,128)(2,1)}, u32[]{:S(2)}, u32[]{:S(2)}) %all-to-all-start.1) | async-done | bytes 5242912 | tf_op jit(solution)/shard_map/all_to_all | solution.py:113
  473.2 5.1 fusion.5
  478.3 7.4 %gather_fusion.1 = bf16[256,4096]{1,0:T(8,128)(2,1)} fusion(bf16[4,80,4096]{2,1,0:T(8,128)(2,1)} %fusion.5, s32[256]{0:T(256)S(1)} %bitcast.220), kind=kCustom, calls=%fused_computation.1 | custom fusion | bytes 4196352 | tf_op jit(solution)/shard_map/gather | solution.py:118
  485.7 5.4 %reshape.411 = f32[128,2,4096]{2,1,0:T(2,128)} reshape(bf16[256,4096]{1,0:T(8,128)(2,1)} %gather_fusion.1) | data formatting | bytes 6291456 | tf_op jit(solution)/shard_map/convert_element_type | solution.py:118
  491.1 8.0 %fusion.30 = (f32[128,1,4096]{2,1,0:T(1,128)S(1)}, f32[128,1,4096]{2,1,0:T(1,128)S(1)}) fusion(f32[128,2,4096]{2,1,0:T(2,128)} %reshape.411), kind=kLoop, calls=%fused_computation.143 | loop fusion | bytes 8388608 | tf_op jit(solution)/shard_map/slice | solution.py:119
  499.2 5.3 %fusion.13 = bf16[1,128,4096]{2,1,0:T(8,128)(2,1)} fusion(f32[128,1,4096]{2,1,0:T(1,128)S(1)} %get-tuple-element.160, f32[128,1,4096]{2,1,0:T(1,128)S(1)} %get-tuple-element.159, bf16[1,128,4096]{2,1,0:T(8,128)(2,1)S(1)} %copy-done.4, f32[16,8,4096]{2,1,0:T(8,128)S(1)} %copy-done.3, f32[128]{0:T(128)S(1)} %get-tuple-element.79, ...), kind=kLoop, calls=%fused_computation.86 | loop fusion | flops 5242880 | bytes 8406016 | tf_op jit(solution)/shard_map/convert_element_type | solution.py:120
  (188 shorter events, 29.7 us)
Async XLA Ops:
  6.5 1.6 copy-start
  6.5 212.3 %all-gather.3.cloned.1.call-start = ((), (), s32[]{:S(2)}) async-start(), calls=%async_computation.2 | async-start | bytes 6553600 | tf_op jit(solution)/shard_map/all_gather | solution.py:102
  12.9 4.8 copy-start.5
  16.4 1.3 copy-start.2
  17.8 3.5 copy-start.11
  21.3 5.3 %copy-start.8 = (f32[128,16]{1,0:T(8,128)}, f32[128,16]{1,0:T(8,128)S(1)}, u32[]{:S(2)}) copy-start(f32[128,16]{1,0:T(8,128)S(1)} %copy.45) | copy-start | bytes 24580
  21.3 2.8 copy-start.6
  26.9 6.7 %copy-start.10 = (f32[16,512]{1,0:T(8,128)S(1)}, f32[16,512]{1,0:T(8,128)}, u32[]{:S(2)}) copy-start(f32[16,512]{1,0:T(8,128)} %get-tuple-element.86) | copy-start | bytes 98308
  33.7 3.5 collective-permute-start
  37.2 13.3 %collective-permute-start = (f32[16,4096]{1,0:T(8,128)S(1)}, f32[16,4096]{1,0:T(8,128)S(1)}, u32[]{:S(2)}, u32[]{:S(2)}) collective-permute-start(f32[16,4096]{1,0:T(8,128)S(1)} %multiply_add_fusion.12), channel_id=1, source_target_pairs={{0,8},{8,16},{16,24},{1,9},{9,17},{17,25},{2,10},{10,18},{18,26},{... | collective-permute-start | bytes 786440 | tf_op jit(solution)/shard_map/while/body/eval_jaxpr/ppermute | solution.py:10
  50.6 7.7 %collective-permute-start = (f32[16,4096]{1,0:T(8,128)S(1)}, f32[16,4096]{1,0:T(8,128)S(1)}, u32[]{:S(2)}, u32[]{:S(2)}) collective-permute-start(f32[16,4096]{1,0:T(8,128)S(1)} %multiply_add_fusion.12), channel_id=1, source_target_pairs={{0,8},{8,16},{16,24},{1,9},{9,17},{17,25},{2,10},{10,18},{18,26},{... | collective-permute-start | bytes 786440 | tf_op jit(solution)/shard_map/while/body/eval_jaxpr/ppermute | solution.py:10
  58.3 73.1 %copy-start.12 = (s32[1,128,2]{1,2,0:T(2,128)S(1)}, s32[1,128,2]{1,2,0:T(2,128)}, u32[]{:S(2)}) copy-start(s32[1,128,2]{1,2,0:T(2,128)} %param.23) | copy-start | bytes 3076
  58.3 75.3 %copy-start.4 = (bf16[1,128,4096]{2,1,0:T(8,128)(2,1)S(1)}, bf16[1,128,4096]{2,1,0:T(8,128)(2,1)}, u32[]{:S(2)}) copy-start(bf16[1,128,4096]{2,1,0:T(8,128)(2,1)} %param.15) | copy-start | bytes 3145732
  58.3 75.3 %copy-start.7 = (f32[4096]{0:T(1024)S(1)}, f32[4096]{0:T(1024)}, u32[]{:S(2)}) copy-start(f32[4096]{0:T(1024)} %param.21) | copy-start | bytes 49156
  212.2 120.0 %all-to-all-start = ((bf16[8,80,4096]{2,1,0:T(8,128)(2,1)}), bf16[8,80,4096]{2,1,0:T(8,128)(2,1)}, u32[]{:S(2)}, u32[]{:S(2)}) async-start(bf16[8,80,4096]{2,1,0:T(8,128)(2,1)} %bitcast.219), calls=%async_computation | async-start | bytes 10485760 | tf_op jit(solution)/shard_map/all_to_all | solution.py:99
  218.0 122.5 %all-gather.5.cloned.1.call-start = ((), (), s32[]{:S(2)}) async-start(), calls=%async_computation.3 | async-start | bytes 6553600 | tf_op jit(solution)/shard_map/all_gather | solution.py:108
  349.0 7.0 %copy-start.9 = (bf16[4,4096]{1,0:T(4,128)(2,1)S(1)}, bf16[4,4096]{1,0:T(4,128)(2,1)}, u32[]{:S(2)}) copy-start(bf16[4,4096]{1,0:T(4,128)(2,1)} %param.22) | copy-start | bytes 98308
  349.0 124.2 %all-to-all-start.1 = ((bf16[8,80,4096]{2,1,0:T(8,128)(2,1)}), bf16[8,80,4096]{2,1,0:T(8,128)(2,1)}, u32[]{:S(2)}, u32[]{:S(2)}) async-start(bf16[8,80,4096]{2,1,0:T(8,128)(2,1)} %bitcast.222), calls=%async_computation.1 | async-start | bytes 10485760 | tf_op jit(solution)/shard_map/all_to_all | solution.py:113
  491.1 8.0 %copy-start.3 = (f32[16,8,4096]{2,1,0:T(8,128)S(1)}, f32[16,8,4096]{2,1,0:T(8,128)}, u32[]{:S(2)}) copy-start(f32[16,8,4096]{2,1,0:T(8,128)} %get-tuple-element.70) | copy-start | bytes 6291460
  499.2 5.3 %copy-start.1 = (bf16[256,4096]{1,0:T(8,128)(2,1)S(1)}, bf16[256,4096]{1,0:T(8,128)(2,1)}, u32[]{:S(2)}) copy-start(bf16[256,4096]{1,0:T(8,128)(2,1)} %param.18) | copy-start | bytes 6291460
Sparse Core Ops, SparseCore 0:
  8.9 43.1 all-gather.2
  220.4 47.2 all-gather.4
where the time goes:
time: 513 us; the launch traced here: 511 us
  waiting for transfers between devices  232 us (45%)
  local copies, waits for them, and re-layouts  160 us (31%)
  other arithmetic  49 us (10%)
  starting transfers between devices  34 us (7%)
  matrix products  22 us (4%)
  between operations  13.7 us (3%)
    all_to_all x1, waiting for transfers between devices, per_device(): lax.all_to_all(partial_out, 'exp', split_axis=0, concat_axis=0, tiled=True)  114 us
    all_to_all x1, waiting for transfers between devices, per_device(): lax.all_to_all(outgoing, 'exp', split_axis=0, concat_axis=0, tiled=True)  113 us
    scatter x1, local copies, waits for them, and re-layouts, per_device(): buffer = jnp.zeros((experts_count, capacity, channels), jnp.bfloat16).at[...  66.9 us
    slice x16, local copies, waits for them, and re-layouts, advance(): drive[inner][None, :] * b_rows[inner][:, None]  38.5 us
    ppermute x3, starting transfers between devices, from_behind(): return lax.ppermute(value, axis, pairs)  21.1 us
    reduce_sum x48, other arithmetic, advance(): results.append(jnp.sum(c_rows[inner][:, None] * state, axis=0))  19.5 us
    dynamic_update_slice x16, local copies, waits for them, and re-layouts, sweep(): final, results = lax.scan(advance, start_state, inputs)  10.6 us
  transfers between devices with their start and end apart: 7, of which 5 were waited for; matrix products, arithmetic and copies ran while one was open for 37% of the time, Pallas kernels for 0%

commit v1 on v0

v1 whole, which is shorter than its diff:
```python
import functools
import math

import jax
import jax.numpy as jnp
from jax import lax
from jax.experimental import pallas as pl
from jax.experimental.pallas import tpu as pltpu
from jax.sharding import PartitionSpec as P

LANES = 128
LOG2E = 1.0 / math.log(2.0)


def fold(rows):
    sub = lax.broadcasted_iota(jnp.int32, rows[0].shape, 0)
    for bit in (1, 2, 4):
        low = (sub & bit) == 0
        rows = [
            jnp.where(low, a, b) + pltpu.roll(jnp.where(low, b, a), 8 - bit, 0)
            for a, b in zip(rows[0::2], rows[1::2])
        ]
    return rows[0]


def fold_states(value):
    parts = [value[k : k + 8] for k in range(0, value.shape[0], 8)]
    return functools.reduce(jnp.add, parts)


def scan_kernel(
    x_ref, dt_ref, wdt_ref, bias_ref, alog_ref, b_ref, c_ref, y_ref, cum_ref, end_ref, delta_s, driven_s
):
    tokens, channels = x_ref.shape
    tiles = channels // LANES
    v = jnp.dot(dt_ref[...], wdt_ref[...], preferred_element_type=jnp.float32) + bias_ref[...]
    delta = jnp.maximum(v, 0.0) + jnp.log1p(jnp.exp(-jnp.abs(v)))
    delta_s[...] = delta
    driven_s[...] = delta * x_ref[...].astype(jnp.float32)
    rates = [
        -jnp.exp(alog_ref[:, j * LANES : (j + 1) * LANES]) * LOG2E for j in range(tiles)
    ]

    def body(group, carry):
        states, sums = list(carry[0]), list(carry[1])
        base = pl.multiple_of(group * 8, 8)
        partial = [[] for _ in range(tiles)]
        cums = [[] for _ in range(tiles)]
        delta8 = delta_s[pl.ds(base, 8), :]
        driven8 = driven_s[pl.ds(base, 8), :]
        for i in range(8):
            bt = b_ref[base + i]
            ct = c_ref[base + i]
            for j in range(tiles):
                cols = slice(j * LANES, (j + 1) * LANES)
                d = delta8[i : i + 1, cols]
                u = driven8[i : i + 1, cols]
                states[j] = jnp.exp2(rates[j] * d) * states[j] + u * bt
                partial[j].append(fold_states(ct * states[j]))
                sums[j] = sums[j] + d
                cums[j].append(sums[j])
        for j in range(tiles):
            cols = slice(j * LANES, (j + 1) * LANES)
            y_ref[pl.ds(base, 8), cols] = fold(partial[j])
            cum_ref[pl.ds(base, 8), cols] = jnp.concatenate(cums[j], axis=0)
        return tuple(states), tuple(sums)

    nstate = alog_ref.shape[0]
    init = (
        tuple(jnp.zeros((nstate, LANES), jnp.float32) for _ in range(tiles)),
        tuple(jnp.zeros((1, LANES), jnp.float32) for _ in range(tiles)),
    )
    states, _ = lax.fori_loop(0, tokens // 8, body, init)
    for j in range(tiles):
        end_ref[:, j * LANES : (j + 1) * LANES] = states[j]


def mix_kernel(
    x_ref, y_ref, cum_ref, alog_ref, start_ref, c_ref, skip_ref, pack_ref, mixer_ref, packed_ref, y_s
):
    tokens, channels = x_ref.shape
    tiles = channels // LANES
    rates = [
        -jnp.exp(alog_ref[:, j * LANES : (j + 1) * LANES]) * LOG2E for j in range(tiles)
    ]
    starts = [start_ref[:, j * LANES : (j + 1) * LANES] for j in range(tiles)]

    def body(group, carry):
        base = pl.multiple_of(group * 8, 8)
        partial = [[] for _ in range(tiles)]
        cum8 = cum_ref[pl.ds(base, 8), :]
        for i in range(8):
            ct = c_ref[base + i]
            for j in range(tiles):
                cols = slice(j * LANES, (j + 1) * LANES)
                d = cum8[i : i + 1, cols]
                partial[j].append(fold_states(ct * (jnp.exp2(rates[j] * d) * starts[j])))
        for j in range(tiles):
            y_s[pl.ds(base, 8), j * LANES : (j + 1) * LANES] = fold(partial[j])
        return carry

    lax.fori_loop(0, tokens // 8, body, 0)
    mixer = (y_s[...] + y_ref[...] + skip_ref[...] * x_ref[...].astype(jnp.float32)).astype(
        jnp.bfloat16
    )
    mixer_ref[...] = mixer
    packed_ref[...] = jnp.dot(pack_ref[...], mixer, preferred_element_type=jnp.float32).astype(
        jnp.bfloat16
    )


def final_kernel(mixer_ref, back_ref, one_ref, two_ref, w_ref, out_ref):
    back = back_ref[...]
    a = jnp.dot(one_ref[...], back, preferred_element_type=jnp.float32)
    b = jnp.dot(two_ref[...], back, preferred_element_type=jnp.float32)
    first = w_ref[:, 0:1]
    second = w_ref[:, 1:2]
    out_ref[...] = (mixer_ref[...].astype(jnp.float32) + (first * a + second * b)).astype(
        jnp.bfloat16
    )


def whole_spec(*shape):
    return pl.BlockSpec(shape, lambda i: (0,) * len(shape))


def run_scan(x, dt, w_dt, bias, a_log, b_wide, c_wide, span):
    tokens, channels = x.shape
    rank, nstate = dt.shape[1], a_log.shape[0]
    cols = lambda rows: pl.BlockSpec((rows, span), lambda i: (0, i))
    return pl.pallas_call(
        scan_kernel,
        grid=(channels // span,),
        in_specs=[
            cols(tokens),
            whole_spec(tokens, rank),
            cols(rank),
            cols(1),
            cols(nstate),
            whole_spec(tokens, nstate, LANES),
            whole_spec(tokens, nstate, LANES),
        ],
        out_specs=[cols(tokens), cols(tokens), cols(nstate)],
        out_shape=[
            jax.ShapeDtypeStruct((tokens, channels), jnp.float32),
            jax.ShapeDtypeStruct((tokens, channels), jnp.float32),
            jax.ShapeDtypeStruct((nstate, channels), jnp.float32),
        ],
        scratch_shapes=[
            pltpu.VMEM((tokens, span), jnp.float32),
            pltpu.VMEM((tokens, span), jnp.float32),
        ],
        compiler_params=pltpu.CompilerParams(vmem_limit_bytes=32 * 1024 * 1024),
        name="scan_local",
    )(x, dt, w_dt, bias[None], a_log, b_wide, c_wide)


def run_mix(x, y, cum, a_log, start, c_wide, skip, pack, span):
    tokens, channels = x.shape
    nstate, slots = a_log.shape[0], pack.shape[0]
    cols = lambda rows: pl.BlockSpec((rows, span), lambda i: (0, i))
    return pl.pallas_call(
        mix_kernel,
        grid=(channels // span,),
        in_specs=[
            cols(tokens),
            cols(tokens),
            cols(tokens),
            cols(nstate),
            cols(nstate),
            whole_spec(tokens, nstate, LANES),
            cols(1),
            whole_spec(slots, tokens),
        ],
        out_specs=[cols(tokens), cols(slots)],
        out_shape=[
            jax.ShapeDtypeStruct((tokens, channels), jnp.bfloat16),
            jax.ShapeDtypeStruct((slots, channels), jnp.bfloat16),
        ],
        scratch_shapes=[pltpu.VMEM((tokens, span), jnp.float32)],
        compiler_params=pltpu.CompilerParams(vmem_limit_bytes=32 * 1024 * 1024),
        name="mix_pack",
    )(x, y, cum, a_log, start, c_wide, skip[None], pack)


def run_final(mixer, back, one, two, weights, span):
    tokens, channels = mixer.shape
    slots = back.shape[0]
    cols = lambda rows: pl.BlockSpec((rows, span), lambda i: (0, i))
    return pl.pallas_call(
        final_kernel,
        grid=(channels // span,),
        in_specs=[
            cols(tokens),
            cols(slots),
            whole_spec(tokens, slots),
            whole_spec(tokens, slots),
            whole_spec(tokens, 2),
        ],
        out_specs=cols(tokens),
        out_shape=jax.ShapeDtypeStruct((tokens, channels), jnp.bfloat16),
        compiler_params=pltpu.CompilerParams(vmem_limit_bytes=32 * 1024 * 1024),
        name="final_sum",
    )(mixer, back, one, two, weights)


def shift(value, by):
    count = lax.axis_size("seq")
    return lax.ppermute(value, "seq", [(i, i + by) for i in range(count - by)])


def carry_in(a_neg, total, end_state):
    count = lax.axis_size("seq")
    both = jnp.concatenate([end_state, total], axis=0)
    start = jnp.zeros_like(end_state)
    between = jnp.zeros_like(total)
    if count <= 4:
        arrived = [shift(both, by) for by in range(1, count)]
        for item in arrived:
            start = start + jnp.exp(a_neg * between) * item[:-1]
            between = between + item[-1:]
        return start

    def relay(index, incoming):
        return shift(jnp.exp(a_neg * total) * incoming + end_state, 1)

    return lax.fori_loop(0, count - 1, relay, start)


def routing(picks, groups, rows):
    tokens = picks.shape[0]
    flat = picks.reshape(-1)
    onehot = (flat[:, None] == jnp.arange(groups, dtype=jnp.int32)[None, :]).astype(jnp.float32)
    steps = jnp.arange(2 * tokens, dtype=jnp.int32)
    earlier = (steps[:, None] > steps[None, :]).astype(jnp.float32)
    before = jnp.dot(earlier, onehot, preferred_element_type=jnp.float32)
    position = jnp.sum(onehot * before, axis=1).astype(jnp.int32)
    place = (flat * rows + position).reshape(tokens, 2)
    slots = jnp.arange(groups * rows, dtype=jnp.int32)
    one = (place[:, 0:1] == slots[None, :]).astype(jnp.bfloat16)
    two = (place[:, 1:2] == slots[None, :]).astype(jnp.bfloat16)
    pack = (
        (place[:, 0][None, :] == slots[:, None]) | (place[:, 1][None, :] == slots[:, None])
    ).astype(jnp.bfloat16)
    return one, two, pack


def per_device(
    x_act, dt_low, b_c, w_dt, dt_bias, a_log, d_skip, w_router, expert_ids, w_up, w_down
):
    x, dt = x_act[0], dt_low[0]
    tokens, channels = x.shape
    nstate = a_log.shape[0]
    groups = w_router.shape[0]
    owners = lax.axis_size("exp")
    capacity = 5 * tokens // owners
    rows = -(-capacity // 16) * 16
    span = 512
    picks = expert_ids[0]
    up = lax.all_gather(w_up, "seq", axis=1, tiled=True)[0]
    down = lax.all_gather(w_down, "seq", axis=2, tiled=True)[0]
    one, two, pack = routing(picks, groups, rows)
    wide = jnp.broadcast_to(b_c[0][:, :, None], b_c.shape[1:] + (LANES,))
    b_wide, c_wide = wide[:, :nstate], wide[:, nstate:]
    y, cum, end_state = run_scan(x, dt, w_dt, dt_bias, a_log, b_wide, c_wide, span)
    start = carry_in(-jnp.exp(a_log), cum[-1:], end_state)
    mixer, packed = run_mix(x, y, cum, a_log, start, c_wide, d_skip, pack, span)

    logits = jnp.dot(mixer, w_router.T, preferred_element_type=jnp.float32)
    ids = jnp.arange(groups, dtype=jnp.int32)
    gap = jnp.sum(
        jnp.where(picks[:, 0:1] == ids, logits, 0.0) - jnp.where(picks[:, 1:2] == ids, logits, 0.0),
        axis=1,
        keepdims=True,
    )
    first = jax.nn.sigmoid(gap)
    weights = jnp.concatenate([first, 1.0 - first], axis=1)

    lanes = [[2 * g + h for g in range(groups)] for h in range(2)]
    swap = [(i, i ^ 1) for i in range(owners)]
    exchange = functools.partial(
        lax.all_to_all, axis_name="exp", split_axis=0, concat_axis=0, axis_index_groups=lanes, tiled=True
    )

    def half(block):
        hidden = jnp.dot(block, up, preferred_element_type=jnp.float32)
        hidden = jax.nn.silu(hidden).astype(jnp.bfloat16)
        return jnp.dot(hidden, down, preferred_element_type=jnp.float32).astype(jnp.bfloat16)

    mine = exchange(packed.reshape(groups, rows, channels)).reshape(-1, channels)
    other = lax.ppermute(mine, "exp", swap)
    theirs = lax.ppermute(half(other), "exp", swap)
    combined = (half(mine).astype(jnp.float32) + theirs.astype(jnp.float32)).astype(jnp.bfloat16)
    back = exchange(combined.reshape(groups, rows, channels)).reshape(-1, channels)
    return run_final(mixer, back, one, two, weights, span)[None]


def solution(mesh):
    in_specs = (
        P("exp", "seq", None),
        P("exp", "seq", None),
        P("exp", "seq", None),
        P(),
        P(),
        P(),
        P(),
        P(),
        P("exp", "seq", None),
        P("exp", "seq", None),
        P("exp", None, "seq"),
    )
    out_specs = P("exp", "seq", None)
    return jax.shard_map(
        per_device, mesh=mesh, in_specs=in_specs, out_specs=out_specs, check_vma=False
    )
```

time: 513 us -> 349 us (0.68)
  local copies, waits for them, and re-layouts: 160 us -> 10.4 us
  blocking collectives: 0 us -> 64.5 us
  other arithmetic: 49 us -> 2.33 us
  waiting for transfers between devices: 232 us -> 191 us
  Pallas kernels: 0 us -> 32.1 us
  starting transfers between devices: 34 us -> 16.3 us
    all_to_all x2 -> x1, waiting for transfers between devices: 227 us -> 55 us  [per_device(): exchange(combined.reshape(groups, rows, channels)).reshape(-1, channels)]
    ppermute x3 -> x5, waiting for transfers between devices: 3.37 us -> 135 us  [the longest x1 56.5 us: per_device(): other = lax.ppermute(mine, 'exp', swap)]
    scatter x1 -> x0, local copies, waits for them, and re-layouts: 66.9 us -> none  [per_device(): buffer = jnp.zeros((experts_count, capacity, channels), jnp.bfloat16).at[...]
    all_to_all x0 -> x1, blocking collectives: none -> 64.5 us  [per_device(): exchange(packed.reshape(groups, rows, channels)).reshape(-1, channels)]
    slice x26 -> x6, local copies, waits for them, and re-layouts: 51 us -> 1.28 us  [the longest x3 0.92 us: per_device(): b_wide, c_wide = (wide[:, :nstate], wide[:, nstate:])]
    pallas_call x0 -> x3, Pallas kernels: none -> 32.1 us  [the longest x1 16 us: run_scan(): pl.pallas_call(scan_kernel, grid=(channels // span,), in_specs=[cols(toke...]
    reduce_sum x51 -> x0, other arithmetic: 28.7 us -> none  [the longest x48 19.5 us: advance(): results.append(jnp.sum(c_rows[inner][:, None] * state, axis=0))]
    gather x6 -> x0, local copies, waits for them, and re-layouts: 13.4 us -> none  [the longest x1 7.38 us: per_device(): combined[flat_ids, position].reshape(tokens_here, 2, channels)]
  transfers between devices with their start and end apart: 7 -> 8, of which waited for: 5 -> 5; matrix products, arithmetic and copies ran while one was open for 37% -> 4% of each run, Pallas kernels for 0% -> 8%
where the time goes in v1:
time: 349 us; the launch traced here: 348 us
  waiting for transfers between devices  191 us (55%)
  blocking collectives  64.5 us (18%)
  Pallas kernels  32.1 us (9%)
  matrix products  18.3 us (5%)
  starting transfers between devices  16.3 us (5%)
  between operations  13.7 us (4%)
  local copies, waits for them, and re-layouts  10.4 us (3%)
    all_to_all x1, blocking collectives, per_device(): exchange(packed.reshape(groups, rows, channels)).reshape(-1, channels)  64.5 us
    ppermute x1, waiting for transfers between devices, per_device(): other = lax.ppermute(mine, 'exp', swap)  56.5 us
    all_to_all x1, waiting for transfers between devices, per_device(): exchange(combined.reshape(groups, rows, channels)).reshape(-1, channels)  55 us
    ppermute x1, waiting for transfers between devices, per_device(): theirs = lax.ppermute(half(other), 'exp', swap)  53.2 us
    ppermute x3, waiting for transfers between devices, shift(): return lax.ppermute(value, 'seq', [(i, i + by) for i in range(count - by)])  25.1 us
    pallas_call x1, Pallas kernels, run_scan(): pl.pallas_call(scan_kernel, grid=(channels // span,), in_specs=[cols(toke...  16 us
    pallas_call x1, Pallas kernels, run_mix(): pl.pallas_call(mix_kernel, grid=(channels // span,), in_specs=[cols(token...  11.7 us
    ppermute x3, starting transfers between devices, shift(): return lax.ppermute(value, 'seq', [(i, i + by) for i in range(count - by)])  9.6 us
  transfers between devices with their start and end apart: 8, of which 5 were waited for; matrix products, arithmetic and copies ran while one was open for 4% of the time, Pallas kernels for 8%

profile of v1, /device:TPU:0, one launch (start us, length us, event | category | flops | bytes accessed | tf_op | source)
XLA Modules:
  0.0 348.2 jit_solution(7714477497332651453)
XLA Ops:
  6.5 0.0 copy-start
  6.5 0.0 all-gather.3.cloned.1.call-start
  6.6 0.7 all-gather.3.cloned.1.call-update
  7.3 0.0 all-gather.5.cloned.1.call-start
  7.3 0.7 fusion.20
  8.0 0.1 copy.29
  8.1 0.1 copy.28
  8.3 0.3 broadcast_in_dim.36.c_ref
  8.6 0.3 broadcast_in_dim.35.b_ref
  8.9 0.0 copy-done.3
  8.9 0.0 copy-done.10
  8.9 0.0 copy-done.11
  9.0 0.0 copy-done.4
  9.0 0.9 copy-done.7
  9.8 16.0 %scan_local.1 = (f32[128,4096]{1,0:T(8,128)S(1)}, f32[128,4096]{1,0:T(8,128)S(1)}, f32[16,4096]{1,0:T(8,128)S(1)}) custom-call(bf16[128,4096]{1,0:T(8,128)(2,1)S(1)} %bitcast.41, bf16[128,256]{1,0:T(8,128)(2,1)S(1)} %bitcast.44, bf16[256,4096]{1,0:T(8,128)(2,1)S(1)} %copy-done.7, f32[1,4096]{1,0:T(1,128)S(1)} %bitcast.45, f32[16,4096]{1,0:T(8,128)S(1)} %copy-done.4, ...), custom_call_target="tpu_custom_call" | custom-call | tf_op jit(solution)/shard_map/scan_local/pallas_call | solution.py:131
  25.8 0.0 copy-start.8
  25.9 1.3 copy-done.8
  27.2 0.0 copy-start.5
  27.2 1.3 copy-done.5
  28.6 2.4 collective-permute-start
  31.0 5.2 %collective-permute-start.1 = (f32[17,4096]{1,0:T(8,128)S(1)}, f32[17,4096]{1,0:T(8,128)}, u32[]{:S(2)}, u32[]{:S(2)}) collective-permute-start(f32[17,4096]{1,0:T(8,128)S(1)} %pad_maximum_fusion), channel_id=1, source_target_pairs={{0,16},{8,24},{1,17},{9,25},{2,18},{10,26},{3,19},{11,27},{4,20},{... | collective-permute-start | bytes 835592 | tf_op jit(solution)/shard_map/ppermute | solution.py:209
  36.1 2.0 collective-permute-start.2
  38.2 0.0 all-gather.5.cloned.1.call-update
  38.2 0.0 copy-done.13
  38.2 0.1 copy.30
  38.3 0.1 eq.101
  38.5 0.2 fusion.7
  38.7 0.1 convert_element_type.40
  38.8 0.2 slice_reduce_fusion.3
  39.1 0.0 collective-permute-done
  39.1 14.2 %collective-permute-done.1 = f32[17,4096]{1,0:T(8,128)} collective-permute-done((f32[17,4096]{1,0:T(8,128)S(1)}, f32[17,4096]{1,0:T(8,128)}, u32[]{:S(2)}, u32[]{:S(2)}) %collective-permute-start.1) | collective-permute-done | bytes 278560 | tf_op jit(solution)/shard_map/ppermute | solution.py:209
  53.2 0.9 fusion.19
  54.2 11.0 %collective-permute-done.2 = f32[17,4096]{1,0:T(8,128)} collective-permute-done((f32[17,4096]{1,0:T(8,128)S(1)}, f32[17,4096]{1,0:T(8,128)}, u32[]{:S(2)}, u32[]{:S(2)}) %collective-permute-start.2) | collective-permute-done | bytes 278560 | tf_op jit(solution)/shard_map/ppermute | solution.py:209
  65.1 1.2 fusion.12.start_ref
  66.3 0.0 copy-done.12
  66.3 0.0 copy-start.6
  66.4 1.6 copy-done.6
  67.9 1.6 copy-done.9
  69.5 11.7 %mix_pack.1 = (bf16[128,4096]{1,0:T(8,128)(2,1)S(1)}, bf16[320,4096]{1,0:T(8,128)(2,1)S(1)}) custom-call(bf16[128,4096]{1,0:T(8,128)(2,1)S(1)} %bitcast.42, f32[128,4096]{1,0:T(8,128)S(1)} %copy-done.9, f32[128,4096]{1,0:T(8,128)S(1)} %copy-done.6, f32[16,4096]{1,0:T(8,128)S(1)} %copy-done.4, f32[16,4096]{1,0:T(8,128)S(1)} %fusion.12.start_ref, ...), custom_call_target="tpu_custom_call" | custom-call | tf_op jit(solution)/shard_map/mix_pack/pallas_call | solution.py:162
  81.3 0.0 copy-start.1
  81.3 64.5 %all_to_all.10 = bf16[4,80,4096]{2,1,0:T(8,128)(2,1)S(1)} all-to-all(bf16[4,80,4096]{2,1,0:T(8,128)(2,1)S(1)} %bitcast.43), channel_id=1, replica_groups={{0,2,4,6},{1,3,5,7},{8,10,12,14},{9,11,13,15},{16,18,20,22},{17,19,21,2..., dimensions={0} | all-to-all | bytes 5242880 | tf_op jit(solution)/shard_map/all_to_all | solution.py:290
  145.8 0.0 copy-done.1
  145.8 1.5 collective-permute-start.3
  147.2 56.5 %collective-permute-done.3 = bf16[320,4096]{1,0:T(8,128)(2,1)} collective-permute-done((bf16[320,4096]{1,0:T(8,128)(2,1)S(1)}, bf16[320,4096]{1,0:T(8,128)(2,1)}, u32[]{:S(2)}, u32[]{:S(2)}) %collective-permute-start.3) | collective-permute-done | bytes 2621472 | tf_op jit(solution)/shard_map/ppermute | solution.py:291
  203.8 5.5 %multiply_convert_fusion = bf16[320,640]{1,0:T(8,128)(2,1)S(1)} fusion(bf16[320,4096]{1,0:T(8,128)(2,1)} %collective-permute-done.3, bf16[1,4096,640]{2,1,0:T(8,128)(2,1)} %all-gather.3.cloned.1.call-done), kind=kOutput, calls=%fused_computation.12 | convolution fusion | flops 1678745600 | bytes 8273920 | tf_op jit(solution)/shard_map/dot_general | solution.py:286
  209.3 0.0 all-gather.5.cloned.1.call-done
  209.3 0.0 copy-start.14
  209.3 0.0 slice-start
  209.3 4.8 %convolution_convert_fusion = bf16[320,4096]{1,0:T(8,128)(2,1)S(1)} fusion(bf16[320,640]{1,0:T(8,128)(2,1)S(1)} %multiply_convert_fusion, bf16[1,640,4096]{2,1,0:T(8,128)(2,1)} %all-gather.5.cloned.1.call-done), kind=kOutput, calls=%fused_computation | convolution fusion | flops 1679032320 | bytes 8273920 | tf_op jit(solution)/shard_map/dot_general | solution.py:288
  214.2 0.0 slice-start.1
  214.2 1.5 collective-permute-start.4
  215.7 0.0 copy-done.14
  215.7 2.3 multiply_convert_fusion.1
  218.1 53.2 %collective-permute-done.4 = bf16[320,4096]{1,0:T(8,128)(2,1)S(1)} collective-permute-done((bf16[320,4096]{1,0:T(8,128)(2,1)S(1)}, bf16[320,4096]{1,0:T(8,128)(2,1)S(1)}, u32[]{:S(2)}, u32[]{:S(2)}) %collective-permute-start.4) | collective-permute-done | bytes 2621472 | tf_op jit(solution)/shard_map/ppermute | solution.py:292
  271.2 0.0 slice-done
  271.2 3.8 %add_convert_fusion = bf16[320,4096]{1,0:T(8,128)(2,1)} fusion(bf16[320,4096]{1,0:T(8,128)(2,1)S(1)} %collective-permute-done.4, bf16[320,640]{1,0:T(8,128)(2,1)S(1)} %multiply_convert_fusion.1, bf16[1,640,4096]{2,1,0:T(8,128)(2,1)S(1)} %bitcast.55), kind=kOutput, calls=%fused_computation.9 | convolution fusion | flops 1684275200 | bytes 10895360 | tf_op jit(solution)/shard_map/dot_general | solution.py:288
  275.0 3.7 %all-to-all-start.1 = ((bf16[4,80,4096]{2,1,0:T(8,128)(2,1)}), bf16[4,80,4096]{2,1,0:T(8,128)(2,1)S(1)}, u32[]{:S(2)}, u32[]{:S(2)}) async-start(bf16[4,80,4096]{2,1,0:T(8,128)(2,1)} %bitcast.47), calls=%async_computation.1 | async-start | bytes 5242880 | tf_op jit(solution)/shard_map/all_to_all | solution.py:294
  278.7 0.2 slice_reduce_fusion.1
  278.8 0.1 fusion.14
  279.0 1.6 subtract_reduce_fusion
  280.6 0.1 copy.32.w_ref
  280.8 55.0 %all-to-all-done.1 = bf16[4,80,4096]{2,1,0:T(8,128)(2,1)S(1)} async-done(((bf16[4,80,4096]{2,1,0:T(8,128)(2,1)}), bf16[4,80,4096]{2,1,0:T(8,128)(2,1)S(1)}, u32[]{:S(2)}, u32[]{:S(2)}) %all-to-all-start.1) | async-done | bytes 2621472 | tf_op jit(solution)/shard_map/all_to_all | solution.py:294
  335.8 1.2 copy-done.2
  337.0 4.4 %final_sum.1 = bf16[128,4096]{1,0:T(8,128)(2,1)} custom-call(bf16[128,4096]{1,0:T(8,128)(2,1)S(1)} %copy-done.2, bf16[320,4096]{1,0:T(8,128)(2,1)S(1)} %bitcast.40, bf16[128,320]{1,0:T(8,128)(2,1)S(1)} %get-tuple-element.23.one_ref, bf16[128,320]{1,0:T(8,128)(2,1)S(1)} %get-tuple-element.24.two_ref, f32[128,2]{1,0:T(8,128)S(1)} %copy.32.w_ref), custom_call_target="tpu_custom_call" | custom-call | tf_op jit(solution)/shard_map/final_sum/pallas_call | solution.py:190
  (21 shorter events, 0.1 us)
Async XLA Ops:
  6.5 272.4 %copy-start = (bf16[4,4096]{1,0:T(4,128)(2,1)S(1)}, bf16[4,4096]{1,0:T(4,128)(2,1)}, u32[]{:S(2)}) copy-start(bf16[4,4096]{1,0:T(4,128)(2,1)} %param.18) | copy-start | bytes 98308
  6.5 2.4 copy-start.3
  6.5 2.4 copy-start.10
  6.5 2.4 copy-start.11
  6.5 2.4 copy-start.4
  6.5 197.2 %all-gather.3.cloned.1.call-start = ((), (), s32[]{:S(2)}) async-start(), calls=%async_computation.2 | async-start | bytes 6553600 | tf_op jit(solution)/shard_map/all_gather | solution.py:260
  7.3 202.0 %all-gather.5.cloned.1.call-start = ((), (), s32[]{:S(2)}) async-start(), calls=%async_computation.3 | async-start | bytes 6553600 | tf_op jit(solution)/shard_map/all_gather | solution.py:261
  8.2 1.6 copy-start.7
  9.8 28.4 %copy-start.13 = (s32[1,128,2]{1,2,0:T(2,128)S(1)}, s32[1,128,2]{1,2,0:T(2,128)}, u32[]{:S(2)}) copy-start(s32[1,128,2]{1,2,0:T(2,128)} %param.19) | copy-start | bytes 3076
  25.8 1.3 copy-start.8
  27.2 39.2 %copy-start.12 = (f32[4096]{0:T(1024)S(1)}, f32[4096]{0:T(1024)}, u32[]{:S(2)}) copy-start(f32[4096]{0:T(1024)} %param.17) | copy-start | bytes 49156
  27.2 1.3 copy-start.5
  28.6 10.5 %collective-permute-start = (f32[17,4096]{1,0:T(8,128)S(1)}, f32[17,4096]{1,0:T(8,128)S(1)}, u32[]{:S(2)}, u32[]{:S(2)}) collective-permute-start(f32[17,4096]{1,0:T(8,128)S(1)} %pad_maximum_fusion), channel_id=1, source_target_pairs={{0,8},{8,16},{16,24},{1,9},{9,17},{17,25},{2,10},{10,18},{18,26},{... | collective-permute-start | bytes 835592 | tf_op jit(solution)/shard_map/ppermute | solution.py:209
  31.0 22.3 %collective-permute-start.1 = (f32[17,4096]{1,0:T(8,128)S(1)}, f32[17,4096]{1,0:T(8,128)}, u32[]{:S(2)}, u32[]{:S(2)}) collective-permute-start(f32[17,4096]{1,0:T(8,128)S(1)} %pad_maximum_fusion), channel_id=1, source_target_pairs={{0,16},{8,24},{1,17},{9,25},{2,18},{10,26},{3,19},{11,27},{4,20},{... | collective-permute-start | bytes 835592 | tf_op jit(solution)/shard_map/ppermute | solution.py:209
  36.1 29.0 %collective-permute-start.2 = (f32[17,4096]{1,0:T(8,128)S(1)}, f32[17,4096]{1,0:T(8,128)}, u32[]{:S(2)}, u32[]{:S(2)}) collective-permute-start(f32[17,4096]{1,0:T(8,128)S(1)} %pad_maximum_fusion), channel_id=1, source_target_pairs={{0,24},{1,25},{2,26},{3,27},{4,28},{5,29},{6,30},{7,31}} | collective-permute-start | bytes 835592 | tf_op jit(solution)/shard_map/ppermute | solution.py:209
  66.3 1.6 copy-start.6
  67.9 1.6 copy-start.9
  81.3 64.5 %copy-start.1 = (bf16[128,4096]{1,0:T(8,128)(2,1)}, bf16[128,4096]{1,0:T(8,128)(2,1)S(1)}, u32[]{:S(2)}) copy-start(bf16[128,4096]{1,0:T(8,128)(2,1)S(1)} %get-tuple-element.13.mixer_ref) | copy-start | bytes 3145732
  145.8 58.0 %collective-permute-start.3 = (bf16[320,4096]{1,0:T(8,128)(2,1)S(1)}, bf16[320,4096]{1,0:T(8,128)(2,1)}, u32[]{:S(2)}, u32[]{:S(2)}) collective-permute-start(bf16[320,4096]{1,0:T(8,128)(2,1)S(1)} %bitcast.48), channel_id=1, source_target_pairs={{0,1},{1,0},{2,3},{3,2},{4,5},{5,4},{6,7},{7,6},{8,9},{9,8},{10,11... | collective-permute-start | bytes 7864328 | tf_op jit(solution)/shard_map/ppermute | solution.py:291
  209.3 6.4 %copy-start.14 = (bf16[1,4096,640]{2,1,0:T(8,128)(2,1)S(1)}, bf16[1,4096,640]{2,1,0:T(8,128)(2,1)}, u32[]{:S(2)}) copy-start(bf16[1,4096,640]{2,1,0:T(8,128)(2,1)} %all-gather.3.cloned.1.call-done) | copy-start | bytes 15728644
  209.3 61.9 %slice-start = ((s8[5242880]{0:T(1024)(128)(4,1)}), s8[4194304]{0:T(1024)(128)(4,1)S(1)}, s32[]{:S(2)}) async-start(s8[5242880]{0:T(1024)(128)(4,1)} %bitcast.54), calls=%async_computation.4 | async-start | bytes 8388608
  214.2 57.0 %slice-start.1 = ((s8[5242880]{0:T(1024)(128)(4,1)}), s8[1048576]{0:T(1024)(128)(4,1)S(1)}, s32[]{:S(2)}) async-start(s8[5242880]{0:T(1024)(128)(4,1)} %bitcast.54), calls=%async_computation.5 | async-start | bytes 2097152
  214.2 57.0 %collective-permute-start.4 = (bf16[320,4096]{1,0:T(8,128)(2,1)S(1)}, bf16[320,4096]{1,0:T(8,128)(2,1)S(1)}, u32[]{:S(2)}, u32[]{:S(2)}) collective-permute-start(bf16[320,4096]{1,0:T(8,128)(2,1)S(1)} %convolution_convert_fusion), channel_id=1, source_target_pairs={{0,1},{1,0},{2,3},{3,2},{4,5},{5,4},{6,7},{7,6},{8,9},{9,8},{10,11... | collective-permute-start | bytes 7864328 | tf_op jit(solution)/shard_map/ppermute | solution.py:292
  275.0 60.8 %all-to-all-start.1 = ((bf16[4,80,4096]{2,1,0:T(8,128)(2,1)}), bf16[4,80,4096]{2,1,0:T(8,128)(2,1)S(1)}, u32[]{:S(2)}, u32[]{:S(2)}) async-start(bf16[4,80,4096]{2,1,0:T(8,128)(2,1)} %bitcast.47), calls=%async_computation.1 | async-start | bytes 5242880 | tf_op jit(solution)/shard_map/all_to_all | solution.py:294
  335.8 1.2 copy-start.2
Sparse Core Ops, SparseCore 0:
  8.9 53.0 all-gather.2
  63.6 44.2 all-gather.4

commit v2 on v1

--- a/solution.py
+++ b/solution.py
@@ -118,6 +118,225 @@
     out_ref[...] = (mixer_ref[...].astype(jnp.float32) + (first * a + second * b)).astype(
         jnp.bfloat16
     )
+
+
+def expert_kernel(
+    packed_ref, up_ref, down_ref, back_ref,
+    recv, wu, wd, part, theirs, comb,
+    local_sem, z_send, z_recv, f_send, f_recv, p_send, p_recv, r_send, r_recv,
+    wy_send, wy_recv, wc_send, wc_recv,
+):
+    groups, rows, channels = packed_ref.shape
+    shards, depth, hidden_units = wu.shape
+    lines = shards // 2
+    me, here = lax.axis_index("exp"), lax.axis_index("seq")
+    z, h = me // 2, lax.rem(me, 2)
+    y, core = here // 2, lax.rem(here, 2)
+    partner = {"exp": 2 * z + 1 - h}
+    sibling = {"seq": 2 * y + 1 - core}
+    mesh_id = pl.DeviceIdType.MESH
+    weights = ((up_ref, wu), (down_ref, wd))
+
+    def behind(k):
+        return lax.rem(z - k + groups, groups)
+
+    def line_behind(j):
+        return lax.rem(y - j + lines, lines)
+
+    def remote(src, dst, send, recv_sem, device):
+        return pltpu.make_async_remote_copy(
+            src_ref=src, dst_ref=dst, send_sem=send, recv_sem=recv_sem,
+            device_id=device, device_id_type=mesh_id,
+        )
+
+    barrier = pltpu.get_barrier_semaphore()
+    for k in range(1, groups):
+        pl.semaphore_signal(
+            barrier, inc=1, device_id={"exp": 2 * lax.rem(z + k, groups) + h}, device_id_type=mesh_id
+        )
+    for j in range(1, lines):
+        pl.semaphore_signal(
+            barrier, inc=1, device_id={"seq": 2 * lax.rem(y + j, lines) + core}, device_id_type=mesh_id
+        )
+    pl.semaphore_signal(barrier, inc=1, device_id=partner, device_id_type=mesh_id)
+    pl.semaphore_signal(barrier, inc=1, device_id=sibling, device_id_type=mesh_id)
+    pl.semaphore_wait(barrier, groups + lines)
+
+    own_rows = pltpu.make_async_copy(packed_ref.at[z], recv.at[z, h], local_sem.at[0])
+    own_rows.start()
+
+    def z_copy(k):
+        to = lax.rem(z + k, groups)
+        return remote(
+            packed_ref.at[to], recv.at[z, h], z_send.at[k], z_recv.at[z], {"exp": 2 * to + h}
+        )
+
+    def wy_copy(w, j):
+        src, dst = weights[w]
+        to = lax.rem(y + j, lines)
+        return remote(
+            src, dst.at[here], wy_send.at[w, j], wy_recv.at[w, y], {"seq": 2 * to + core}
+        )
+
+    def wc_copy(w, j):
+        src, dst = weights[w]
+        line = line_behind(j)
+        shard = 2 * line + core
+        return remote(
+            src if j == 0 else dst.at[shard], dst.at[shard],
+            wc_send.at[w, j], wc_recv.at[w, line], sibling,
+        )
+
+    def f_copy(k):
+        src = behind(k)
+        return remote(recv.at[src, h], recv.at[src, h], f_send.at[k], f_recv.at[src], partner)
+
+    def p_copy(k):
+        src = behind(k)
+        return remote(part.at[src, 1 - h], theirs.at[src], p_send.at[k], p_recv.at[src], partner)
+
+    def r_copy(k):
+        src = behind(k)
+        return remote(
+            comb.at[src], back_ref.at[z], r_send.at[k], r_recv.at[z], {"exp": 2 * src + h}
+        )
+
+    def wait_into(dst, sem):
+        remote(dst, dst, sem, sem, partner).wait_recv()
+
+    for k in range(1, groups):
+        z_copy(k).start()
+    own_weights = []
+    for w, (src, dst) in enumerate(weights):
+        own = pltpu.make_async_copy(src, dst.at[here], local_sem.at[1 + w])
+        own.start()
+        own_weights.append(own)
+        for j in range(1, lines):
+            wy_copy(w, j).start()
+        wc_copy(w, 0).start()
+
+    def forward(k):
+        src = behind(k)
+        if k == 0:
+            own_rows.wait()
+        else:
+            wait_into(recv.at[src, h], z_recv.at[src])
+        f_copy(k).start()
+
+    def relay_weights(w):
+        dst = weights[w][1]
+        for j in range(1, lines):
+            line = line_behind(j)
+            wait_into(dst.at[2 * line + core], wy_recv.at[w, line])
+            wc_copy(w, j).start()
+
+    def collect_weights(w):
+        dst = weights[w][1]
+        own_weights[w].wait()
+        for j in range(lines):
+            line = line_behind(j)
+            wait_into(dst.at[2 * line + 1 - core], wc_recv.at[w, line])
+
+    def compute(k):
+        src = behind(k)
+        wait_into(recv.at[src, 1 - h], f_recv.at[src])
+
+        def up_step(i, acc):
+            cols = pl.ds(pl.multiple_of(i * depth, depth), depth)
+            block = recv[src, :, :, cols].reshape(2 * rows, depth)
+            return acc + jnp.dot(block, wu[i], preferred_element_type=jnp.float32)
+
+        pre = lax.fori_loop(
+            0, shards, up_step, jnp.zeros((2 * rows, hidden_units), jnp.float32)
+        )
+        hidden = (pre / (1.0 + jnp.exp(-pre))).astype(jnp.bfloat16)
+
+        def down_step(i, carry):
+            cols = pl.ds(pl.multiple_of(i * depth, depth), depth)
+            out = jnp.dot(hidden, wd[i], preferred_element_type=jnp.float32)
+            part[src, :, :, cols] = out.astype(jnp.bfloat16).reshape(2, rows, depth)
+            return carry
+
+        lax.fori_loop(0, shards, down_step, 0)
+        p_copy(k).start()
+
+    def combine(k):
+        src = behind(k)
+        wait_into(theirs.at[src], p_recv.at[src])
+
+        def add(i, carry):
+            cols = pl.ds(pl.multiple_of(i * depth, depth), depth)
+            comb[src, :, cols] = (
+                part[src, h, :, cols].astype(jnp.float32) + theirs[src, :, cols].astype(jnp.float32)
+            ).astype(jnp.bfloat16)
+            return carry
+
+        lax.fori_loop(0, shards, add, 0)
+        if k == 0:
+            pltpu.make_async_copy(comb.at[z], back_ref.at[z], local_sem.at[3]).start()
+        else:
+            r_copy(k).start()
+
+    for k in range(groups - 2):
+        forward(k)
+    relay_weights(0)
+    forward(groups - 2)
+    relay_weights(1)
+    collect_weights(0)
+    collect_weights(1)
+    for k in range(groups):
+        if k == 1:
+            forward(groups - 1)
+        compute(k)
+        if k > 0:
+            combine(k - 1)
+    combine(groups - 1)
+
+    pltpu.make_async_copy(comb.at[z], back_ref.at[z], local_sem.at[3]).wait()
+    for k in range(1, groups):
+        src = behind(k)
+        wait_into(back_ref.at[src], r_recv.at[src])
+        z_copy(k).wait_send()
+        r_copy(k).wait_send()
+    for k in range(groups):
+        f_copy(k).wait_send()
+        p_copy(k).wait_send()
+    for w in range(2):
+        for j in range(lines):
+            if j > 0:
+                wy_copy(w, j).wait_send()
+            wc_copy(w, j).wait_send()
+
+
+def run_experts(packed, w_up, w_down):
+    groups, rows, channels = packed.shape
+    depth, hidden_units = w_up.shape
+    shards = channels // depth
+    lines = shards // 2
+    dma = pltpu.SemaphoreType.DMA
+    any_spec = pl.BlockSpec(memory_space=pl.ANY)
+    bf16 = jnp.bfloat16
+    return pl.pallas_call(
+        expert_kernel,
+        in_specs=[any_spec] * 3,
+        out_specs=any_spec,
+        out_shape=jax.ShapeDtypeStruct(packed.shape, bf16),
+        scratch_shapes=[
+            pltpu.VMEM((groups, 2, rows, channels), bf16),
+            pltpu.VMEM((shards, depth, hidden_units), bf16),
+            pltpu.VMEM((shards, hidden_units, depth), bf16),
+            pltpu.VMEM((groups, 2, rows, channels), bf16),
+            pltpu.VMEM((groups, rows, channels), bf16),
+            pltpu.VMEM((groups, rows, channels), bf16),
+            dma((4,)),
+        ]
+        + [dma((groups,)) for _ in range(8)]
+        + [dma((2, lines)) for _ in range(4)],
+        compiler_params=pltpu.CompilerParams(
+            collective_id=0, has_side_effects=True, vmem_limit_bytes=56 * 1024 * 1024
+        ),
+        name="experts",
+    )(packed, w_up, w_down)
 
 
 def whole_spec(*shape):
@@ -257,8 +476,6 @@
     rows = -(-capacity // 16) * 16
     span = 512
     picks = expert_ids[0]
-    up = lax.all_gather(w_up, "seq", axis=1, tiled=True)[0]
-    down = lax.all_gather(w_down, "seq", axis=2, tiled=True)[0]
     one, two, pack = routing(picks, groups, rows)
     wide = jnp.broadcast_to(b_c[0][:, :, None], b_c.shape[1:] + (LANES,))
     b_wide, c_wide = wide[:, :nstate], wide[:, nstate:]
@@ -276,22 +493,8 @@
     first = jax.nn.sigmoid(gap)
     weights = jnp.concatenate([first, 1.0 - first], axis=1)
 
-    lanes = [[2 * g + h for g in range(groups)] for h in range(2)]
-    swap = [(i, i ^ 1) for i in range(owners)]
-    exchange = functools.partial(
-        lax.all_to_all, axis_name="exp", split_axis=0, concat_axis=0, axis_index_groups=lanes, tiled=True
-    )
-
-    def half(block):
-        hidden = jnp.dot(block, up, preferred_element_type=jnp.float32)
-        hidden = jax.nn.silu(hidden).astype(jnp.bfloat16)
-        return jnp.dot(hidden, down, preferred_element_type=jnp.float32).astype(jnp.bfloat16)
-
-    mine = exchange(packed.reshape(groups, rows, channels)).reshape(-1, channels)
-    other = lax.ppermute(mine, "exp", swap)
-    theirs = lax.ppermute(half(other), "exp", swap)
-    combined = (half(mine).astype(jnp.float32) + theirs.astype(jnp.float32)).astype(jnp.bfloat16)
-    back = exchange(combined.reshape(groups, rows, channels)).reshape(-1, channels)
+    back = run_experts(packed.reshape(groups, rows, channels), w_up[0], w_down[0])
+    back = back.reshape(-1, channels)
     return run_final(mixer, back, one, two, weights, span)[None]
 
 

time: 349 us -> 238 us (0.68)
  waiting for transfers between devices: 191 us -> 9.9 us
  Pallas kernels: 32.1 us -> 203 us
  blocking collectives: 64.5 us -> 0 us
  matrix products: 18.3 us -> 0.59 us
  between operations: 13.7 us -> 0.26 us
  starting transfers between devices: 16.3 us -> 9.6 us
    pallas_call x0 -> x1, Pallas kernels: none -> 171 us  [run_experts(): pl.pallas_call(expert_kernel, in_specs=[any_spec] * 3, out_specs=any_spec...]
    ppermute x2 -> x0, waiting for transfers between devices: 110 us -> none  [the longest x1 56.5 us: per_device(): other = lax.ppermute(mine, 'exp', swap)]
    all_to_all x1 -> x0, blocking collectives: 64.5 us -> none  [per_device(): exchange(packed.reshape(groups, rows, channels)).reshape(-1, channels)]
    all_to_all x1 -> x0, waiting for transfers between devices: 55 us -> none  [per_device(): exchange(combined.reshape(groups, rows, channels)).reshape(-1, channels)]
    dot_general x4 -> x0, matrix products: 16.5 us -> none  [the longest x2 8.61 us: half(): jnp.dot(hidden, down, preferred_element_type=jnp.float32)]
    ppermute x3, waiting for transfers between devices: 25.1 us -> 9.9 us  [shift(): return lax.ppermute(value, 'seq', [(i, i + by) for i in range(count - by)])]
    all_to_all x1 -> x0, starting transfers between devices: 3.65 us -> none  [per_device(): exchange(combined.reshape(groups, rows, channels)).reshape(-1, channels)]
    unnamed x35 -> x31, local copies, waits for them, and re-layouts: 8.09 us -> 9.21 us
  transfers between devices with their start and end apart: 8 -> 3, of which waited for: 5 -> 2; matrix products, arithmetic and copies ran while one was open for 4% -> 1% of each run, Pallas kernels for 8% -> 0%
where the time goes in v2:
time: 238 us
  Pallas kernels  203 us (85%)
  local copies, waits for them, and re-layouts  11.7 us (5%)
  waiting for transfers between devices  9.9 us (4%)
  starting transfers between devices  9.6 us (4%)
  other arithmetic  2.96 us (1%)
    pallas_call x1, Pallas kernels, run_experts(): pl.pallas_call(expert_kernel, in_specs=[any_spec] * 3, out_specs=any_spec...  171 us
    pallas_call x1, Pallas kernels, run_scan(): pl.pallas_call(scan_kernel, grid=(channels // span,), in_specs=[cols(toke...  16 us
    pallas_call x1, Pallas kernels, run_mix(): pl.pallas_call(mix_kernel, grid=(channels // span,), in_specs=[cols(token...  11.7 us
    ppermute x3, waiting for transfers between devices, shift(): return lax.ppermute(value, 'seq', [(i, i + by) for i in range(count - by)])  9.9 us
    ppermute x3, starting transfers between devices, shift(): return lax.ppermute(value, 'seq', [(i, i + by) for i in range(count - by)])  9.6 us
    unnamed x31, local copies, waits for them, and re-layouts  9.21 us
  transfers between devices with their start and end apart: 3, of which 2 were waited for; matrix products, arithmetic and copies ran while one was open for 1% of the time, Pallas kernels for 0%

profile of v2, /device:TPU:0, one launch (start us, length us, event | category | flops | bytes accessed | tf_op | source)
XLA Modules:
  0.0 238.1 jit_solution(5911313500789652622)
XLA Ops:
  0.0 0.0 copy-start
  0.0 0.0 copy-start.2
  0.0 0.0 copy-start.11
  0.0 0.0 copy-start.12
  0.0 0.0 copy-start.4
  0.0 0.8 fusion.9
  0.8 0.1 copy.29
  0.9 0.1 copy.28
  1.0 0.3 broadcast_in_dim.36.c_ref
  1.4 0.3 broadcast_in_dim.35.b_ref
  1.7 0.0 copy-done.2
  1.7 0.0 copy-done.11
  1.7 0.0 copy-done.12
  1.7 0.0 copy-done.4
  1.8 0.0 copy-start.7
  1.8 1.6 copy-done.7
  3.4 0.0 copy-start.14
  3.4 16.0 %scan_local.1 = (f32[128,4096]{1,0:T(8,128)S(1)}, f32[128,4096]{1,0:T(8,128)S(1)}, f32[16,4096]{1,0:T(8,128)S(1)}) custom-call(bf16[128,4096]{1,0:T(8,128)(2,1)S(1)} %bitcast.21, bf16[128,256]{1,0:T(8,128)(2,1)S(1)} %bitcast.24, bf16[256,4096]{1,0:T(8,128)(2,1)S(1)} %copy-done.7, f32[1,4096]{1,0:T(1,128)S(1)} %bitcast.25, f32[16,4096]{1,0:T(8,128)S(1)} %copy-done.4, ...), custom_call_target="tpu_custom_call" | custom-call | tf_op jit(solution)/shard_map/scan_local/pallas_call | solution.py:350
  19.4 0.0 copy-start.8
  19.4 1.3 copy-done.8
  20.7 0.0 copy-start.13
  20.7 0.0 copy-start.5
  20.7 1.3 copy-done.5
  22.1 2.4 %collective-permute-start = (f32[17,4096]{1,0:T(8,128)S(1)}, f32[17,4096]{1,0:T(8,128)S(1)}, u32[]{:S(2)}, u32[]{:S(2)}) collective-permute-start(f32[17,4096]{1,0:T(8,128)S(1)} %pad_maximum_fusion), channel_id=1, source_target_pairs={{0,8},{8,16},{16,24},{1,9},{9,17},{17,25},{2,10},{10,18},{18,26},{... | collective-permute-start | bytes 835592 | tf_op jit(solution)/shard_map/ppermute | solution.py:428
  24.5 5.2 %collective-permute-start.1 = (f32[17,4096]{1,0:T(8,128)S(1)}, f32[17,4096]{1,0:T(8,128)}, u32[]{:S(2)}, u32[]{:S(2)}) collective-permute-start(f32[17,4096]{1,0:T(8,128)S(1)} %pad_maximum_fusion), channel_id=1, source_target_pairs={{0,16},{8,24},{1,17},{9,25},{2,18},{10,26},{3,19},{11,27},{4,20},{... | collective-permute-start | bytes 835592 | tf_op jit(solution)/shard_map/ppermute | solution.py:428
  29.6 2.0 collective-permute-start.2
  31.7 0.0 copy-done.14
  31.7 0.1 copy.30
  31.8 0.1 eq.101
  31.9 0.2 fusion
  32.2 0.1 convert_element_type.19
  32.3 0.0 copy-start.6
  32.3 0.2 slice_reduce_fusion.3
  32.6 0.2 slice_reduce_fusion.1
  32.7 0.7 fusion.3
  33.5 0.0 collective-permute-done
  33.5 5.0 %collective-permute-done.1 = f32[17,4096]{1,0:T(8,128)} collective-permute-done((f32[17,4096]{1,0:T(8,128)S(1)}, f32[17,4096]{1,0:T(8,128)}, u32[]{:S(2)}, u32[]{:S(2)}) %collective-permute-start.1) | collective-permute-done | bytes 278560 | tf_op jit(solution)/shard_map/ppermute | solution.py:428
  38.4 0.9 fusion.8
  39.4 4.9 %collective-permute-done.2 = f32[17,4096]{1,0:T(8,128)} collective-permute-done((f32[17,4096]{1,0:T(8,128)S(1)}, f32[17,4096]{1,0:T(8,128)}, u32[]{:S(2)}, u32[]{:S(2)}) %collective-permute-start.2) | collective-permute-done | bytes 278560 | tf_op jit(solution)/shard_map/ppermute | solution.py:428
  44.3 1.2 fusion.1.start_ref
  45.5 0.0 copy-done.13
  45.5 0.0 copy-done.6
  45.5 0.0 copy-start.9
  45.5 1.6 copy-done.9
  47.1 11.7 %mix_pack.1 = (bf16[128,4096]{1,0:T(8,128)(2,1)S(1)}, bf16[320,4096]{1,0:T(8,128)(2,1)S(1)}) custom-call(bf16[128,4096]{1,0:T(8,128)(2,1)S(1)} %bitcast.22, f32[128,4096]{1,0:T(8,128)S(1)} %copy-done.9, f32[128,4096]{1,0:T(8,128)S(1)} %copy-done.6, f32[16,4096]{1,0:T(8,128)S(1)} %copy-done.4, f32[16,4096]{1,0:T(8,128)S(1)} %fusion.1.start_ref, ...), custom_call_target="tpu_custom_call" | custom-call | tf_op jit(solution)/shard_map/mix_pack/pallas_call | solution.py:381
  58.9 0.0 copy-start.3
  58.9 1.5 copy-done.3
  60.4 0.0 copy-done
  60.4 0.4 subtract_reduce_fusion
  60.8 0.1 copy.32.w_ref
  60.9 0.0 copy-start.10
  60.9 171.0 %experts.1 = bf16[4,80,4096]{2,1,0:T(8,128)(2,1)} custom-call(bf16[4,80,4096]{2,1,0:T(8,128)(2,1)} %bitcast.23, bf16[1024,640]{1,0:T(8,128)(2,1)} %bitcast.28, bf16[640,1024]{1,0:T(8,128)(2,1)} %bitcast.29), custom_call_target="tpu_custom_call" | custom-call | tf_op jit(solution)/shard_map/experts/pallas_call | solution.py:319
  231.9 0.0 copy-done.10
  232.0 0.0 copy-start.1
  232.0 1.7 copy-done.1
  233.7 4.4 %final_sum.1 = bf16[128,4096]{1,0:T(8,128)(2,1)} custom-call(bf16[128,4096]{1,0:T(8,128)(2,1)S(1)} %get-tuple-element.13.mixer_ref, bf16[320,4096]{1,0:T(8,128)(2,1)S(1)} %bitcast.20, bf16[128,320]{1,0:T(8,128)(2,1)S(1)} %get-tuple-element.23.one_ref, bf16[128,320]{1,0:T(8,128)(2,1)S(1)} %copy-done.10, f32[128,2]{1,0:T(8,128)S(1)} %copy.32.w_ref), custom_call_target="tpu_custom_call" | custom-call | tf_op jit(solution)/shard_map/final_sum/pallas_call | solution.py:409
  (8 shorter events, 0.1 us)
Async XLA Ops:
  0.0 60.4 %copy-start = (bf16[4,4096]{1,0:T(4,128)(2,1)S(1)}, bf16[4,4096]{1,0:T(4,128)(2,1)}, u32[]{:S(2)}) copy-start(bf16[4,4096]{1,0:T(4,128)(2,1)} %param.18) | copy-start | bytes 98308
  0.0 1.7 copy-start.2
  0.0 1.7 copy-start.11
  0.0 1.7 copy-start.12
  0.0 1.7 copy-start.4
  1.8 1.6 copy-start.7
  3.4 28.3 %copy-start.14 = (s32[1,128,2]{1,2,0:T(2,128)S(1)}, s32[1,128,2]{1,2,0:T(2,128)}, u32[]{:S(2)}) copy-start(s32[1,128,2]{1,2,0:T(2,128)} %param.19) | copy-start | bytes 3076
  19.4 1.3 copy-start.8
  20.7 24.8 %copy-start.13 = (f32[4096]{0:T(1024)S(1)}, f32[4096]{0:T(1024)}, u32[]{:S(2)}) copy-start(f32[4096]{0:T(1024)} %param.17) | copy-start | bytes 49156
  20.7 1.3 copy-start.5
  22.1 11.4 %collective-permute-start = (f32[17,4096]{1,0:T(8,128)S(1)}, f32[17,4096]{1,0:T(8,128)S(1)}, u32[]{:S(2)}, u32[]{:S(2)}) collective-permute-start(f32[17,4096]{1,0:T(8,128)S(1)} %pad_maximum_fusion), channel_id=1, source_target_pairs={{0,8},{8,16},{16,24},{1,9},{9,17},{17,25},{2,10},{10,18},{18,26},{... | collective-permute-start | bytes 835592 | tf_op jit(solution)/shard_map/ppermute | solution.py:428
  24.5 14.0 %collective-permute-start.1 = (f32[17,4096]{1,0:T(8,128)S(1)}, f32[17,4096]{1,0:T(8,128)}, u32[]{:S(2)}, u32[]{:S(2)}) collective-permute-start(f32[17,4096]{1,0:T(8,128)S(1)} %pad_maximum_fusion), channel_id=1, source_target_pairs={{0,16},{8,24},{1,17},{9,25},{2,18},{10,26},{3,19},{11,27},{4,20},{... | collective-permute-start | bytes 835592 | tf_op jit(solution)/shard_map/ppermute | solution.py:428
  29.6 14.6 %collective-permute-start.2 = (f32[17,4096]{1,0:T(8,128)S(1)}, f32[17,4096]{1,0:T(8,128)}, u32[]{:S(2)}, u32[]{:S(2)}) collective-permute-start(f32[17,4096]{1,0:T(8,128)S(1)} %pad_maximum_fusion), channel_id=1, source_target_pairs={{0,24},{1,25},{2,26},{3,27},{4,28},{5,29},{6,30},{7,31}} | collective-permute-start | bytes 835592 | tf_op jit(solution)/shard_map/ppermute | solution.py:428
  32.3 13.2 %copy-start.6 = (f32[128,4096]{1,0:T(8,128)S(1)}, f32[128,4096]{1,0:T(8,128)}, u32[]{:S(2)}) copy-start(f32[128,4096]{1,0:T(8,128)} %copy-done.5) | copy-start | bytes 6291460
  45.5 1.6 copy-start.9
  58.9 1.5 copy-start.3
  60.9 171.0 %copy-start.10 = (bf16[128,320]{1,0:T(8,128)(2,1)S(1)}, bf16[128,320]{1,0:T(8,128)(2,1)}, u32[]{:S(2)}) copy-start(bf16[128,320]{1,0:T(8,128)(2,1)} %get-tuple-element.24.two_ref) | copy-start | bytes 245764
  232.0 1.7 copy-start.1

commit v3 on v1

--- a/solution.py
+++ b/solution.py
@@ -120,8 +120,237 @@
     )
 
 
+def expert_kernel(
+    packed_ref, up_ref, up_x_ref, up_y_ref, down_ref, back_ref,
+    recv, wu, wd, comb,
+    local_sem, own_sem, up_y_sem, z_send, z_recv, r_send, r_recv,
+    x_send, x_recv, y_send, y_recv, c_send, c_recv,
+):
+    groups, rows, channels = packed_ref.shape
+    _, shards, depth, hidden_units = wu.shape
+    lines = shards // 2
+    me, here = lax.axis_index("exp"), lax.axis_index("seq")
+    z, h = me // 2, lax.rem(me, 2)
+    y, core = here // 2, lax.rem(here, 2)
+    partner = {"exp": 2 * z + 1 - h}
+    sibling = {"seq": 2 * y + 1 - core}
+    mesh_id = pl.DeviceIdType.MESH
+
+    def behind(k):
+        return lax.rem(z - k + groups, groups)
+
+    def line_behind(j):
+        return lax.rem(y - j + lines, lines)
+
+    def line_peer(j):
+        return {"seq": 2 * lax.rem(y + j, lines) + core}
+
+    def remote(src, dst, send, recv_sem, device):
+        return pltpu.make_async_remote_copy(
+            src_ref=src, dst_ref=dst, send_sem=send, recv_sem=recv_sem,
+            device_id=device, device_id_type=mesh_id,
+        )
+
+    def wait_into(dst, sem):
+        remote(dst, dst, sem, sem, partner).wait_recv()
+
+    barrier = pltpu.get_barrier_semaphore()
+    for k in range(1, groups):
+        pl.semaphore_signal(
+            barrier, inc=1, device_id={"exp": 2 * lax.rem(z + k, groups) + h}, device_id_type=mesh_id
+        )
+    for j in range(1, lines):
+        pl.semaphore_signal(barrier, inc=1, device_id=line_peer(j), device_id_type=mesh_id)
+    pl.semaphore_signal(barrier, inc=1, device_id=partner, device_id_type=mesh_id)
+    pl.semaphore_signal(barrier, inc=1, device_id=sibling, device_id_type=mesh_id)
+    pl.semaphore_wait(barrier, groups + lines)
+
+    def z_copy(k):
+        to = lax.rem(z + k, groups)
+        return remote(
+            packed_ref.at[to], recv.at[z], z_send.at[k], z_recv.at[z], {"exp": 2 * to + h}
+        )
+
+    def r_copy(k):
+        src = behind(k)
+        return remote(
+            comb.at[src], back_ref.at[z], r_send.at[k], r_recv.at[z], {"exp": 2 * src + h}
+        )
+
+    def half_of(q):
+        return h if q == 0 else 1 - h
+
+    def y_copy(q, j):
+        src = down_ref if q == 0 else wd.at[1 - h, here]
+        return remote(
+            src, wd.at[half_of(q), here], y_send.at[q, j], y_recv.at[q, y], line_peer(j)
+        )
+
+    def x_copy(j):
+        if j == 0:
+            return remote(down_ref, wd.at[h, here], x_send.at[0], x_recv.at[y], partner)
+        line = line_behind(j)
+        return remote(
+            up_y_ref.at[j - 1], wu.at[h, 2 * line + core], x_send.at[j], x_recv.at[line], partner
+        )
+
+    def c_copy(w, q, j):
+        line = line_behind(j)
+        shard = 2 * line + core
+        dst = (wu if w == 0 else wd).at[half_of(q), shard]
+        if j == 0:
+            src = ((up_ref, up_x_ref), (down_ref, dst))[w][q]
+        elif w == 0 and q == 0:
+            src = up_y_ref.at[j - 1]
+        else:
+            src = dst
+        at = (2 * w + half_of(q)) * lines + line
+        return remote(src, dst, c_send.at[(2 * w + q) * lines + j], c_recv.at[at], sibling)
+
+    for k in range(1, groups):
+        z_copy(k).start()
+    for j in range(1, lines):
+        y_copy(0, j).start()
+    for j in range(lines):
+        x_copy(j).start()
+    local = [
+        pltpu.make_async_copy(packed_ref.at[z], recv.at[z], local_sem.at[0]),
+        pltpu.make_async_copy(up_ref, wu.at[h, here], own_sem.at[0]),
+        pltpu.make_async_copy(up_x_ref, wu.at[1 - h, here], own_sem.at[1]),
+        pltpu.make_async_copy(down_ref, wd.at[h, here], own_sem.at[2]),
+    ]
+    for j in range(1, lines):
+        local.append(
+            pltpu.make_async_copy(
+                up_y_ref.at[j - 1], wu.at[h, 2 * line_behind(j) + core], up_y_sem.at[j]
+            )
+        )
+    for copy in local:
+        copy.start()
+    c_copy(0, 0, 0).start()
+    c_copy(0, 1, 0).start()
+    c_copy(1, 0, 0).start()
+    for j in range(1, lines):
+        c_copy(0, 0, j).start()
+    wait_into(wd.at[1 - h, here], x_recv.at[y])
+    for j in range(1, lines):
+        y_copy(1, j).start()
+    c_copy(1, 1, 0).start()
+    for j in range(1, lines):
+        line = line_behind(j)
+        wait_into(wu.at[1 - h, 2 * line + core], x_recv.at[line])
+        c_copy(0, 1, j).start()
+    for q in range(2):
+        for j in range(1, lines):
+            line = line_behind(j)
+            wait_into(wd.at[half_of(q), 2 * line + core], y_recv.at[q, line])
+            c_copy(1, q, j).start()
+    for copy in local:
+        copy.wait()
+    for w in range(2):
+        for half in range(2):
+            for j in range(lines):
+                line = line_behind(j)
+                wait_into(
+                    (wu if w == 0 else wd).at[half, 2 * line + 1 - core],
+                    c_recv.at[(2 * w + half) * lines + line],
+                )
+
+    def compute(first, second):
+        sources = [behind(first), behind(second)]
+        for k, src in zip((first, second), sources):
+            if k:
+                wait_into(recv.at[src], z_recv.at[src])
+        zero = jnp.zeros((2 * rows, hidden_units), jnp.float32)
+
+        def up_step(i, acc):
+            cols = pl.ds(pl.multiple_of(i * depth, depth), depth)
+            block = jnp.concatenate([recv[src, :, cols] for src in sources], axis=0)
+            return tuple(
+                acc[n] + jnp.dot(block, wu[n, i], preferred_element_type=jnp.float32)
+                for n in range(2)
+            )
+
+        pre = lax.fori_loop(0, shards, up_step, (zero, zero))
+        hidden = [(p / (1.0 + jnp.exp(-p))).astype(jnp.bfloat16) for p in pre]
+
+        def down_step(i, carry):
+            cols = pl.ds(pl.multiple_of(i * depth, depth), depth)
+            total = sum(
+                jnp.dot(hidden[n], wd[n, i], preferred_element_type=jnp.float32)
+                .astype(jnp.bfloat16)
+                .astype(jnp.float32)
+                for n in range(2)
+            ).astype(jnp.bfloat16)
+            for n, src in enumerate(sources):
+                comb[src, :, cols] = total[n * rows : (n + 1) * rows]
+            return carry
+
+        lax.fori_loop(0, shards, down_step, 0)
+        for k in (first, second):
+            if k:
+                r_copy(k).start()
+
+    order = list(range(1, groups)) + [0]
+    for k in range(0, groups, 2):
+        compute(order[k], order[k + 1])
+    keep = pltpu.make_async_copy(comb.at[z], back_ref.at[z], local_sem.at[0])
+    keep.start()
+    keep.wait()
+    for k in range(1, groups):
+        src = behind(k)
+        wait_into(back_ref.at[src], r_recv.at[src])
+        z_copy(k).wait_send()
+        r_copy(k).wait_send()
+    for j in range(lines):
+        x_copy(j).wait_send()
+    for j in range(1, lines):
+        for q in range(2):
+            y_copy(q, j).wait_send()
+    for w in range(2):
+        for q in range(2):
+            for j in range(lines):
+                c_copy(w, q, j).wait_send()
+
+
+def run_experts(packed, w_up, up_x, up_y, w_down):
+    groups, rows, channels = packed.shape
+    depth, hidden_units = w_up.shape
+    shards = channels // depth
+    lines = shards // 2
+    dma = pltpu.SemaphoreType.DMA
+    any_spec = pl.BlockSpec(memory_space=pl.ANY)
+    bf16 = jnp.bfloat16
+    return pl.pallas_call(
+        expert_kernel,
+        in_specs=[any_spec] * 5,
+        out_specs=any_spec,
+        out_shape=jax.ShapeDtypeStruct(packed.shape, bf16),
+        scratch_shapes=[
+            pltpu.VMEM((groups, rows, channels), bf16),
+            pltpu.VMEM((2, shards, depth, hidden_units), bf16),
+            pltpu.VMEM((2, shards, hidden_units, depth), bf16),
+            pltpu.VMEM((groups, rows, channels), bf16),
+            dma((1,)),
+            dma((3,)),
+            dma((lines,)),
+        ]
+        + [dma((groups,)) for _ in range(4)]
+        + [dma((lines,)), dma((lines,)), dma((2, lines)), dma((2, lines))]
+        + [dma((4 * lines,)), dma((4 * lines,))],
+        compiler_params=pltpu.CompilerParams(
+            collective_id=0, has_side_effects=True, vmem_limit_bytes=56 * 1024 * 1024
+        ),
+        name="experts",
+    )(packed, w_up, up_x, up_y, w_down)
+
+
 def whole_spec(*shape):
     return pl.BlockSpec(shape, lambda i: (0,) * len(shape))
+
+
+def vector_cost(updates):
+    return pl.CostEstimate(flops=2048 * updates, bytes_accessed=6 * updates, transcendentals=updates)
 
 
 def run_scan(x, dt, w_dt, bias, a_log, b_wide, c_wide, span):
@@ -151,6 +380,7 @@
             pltpu.VMEM((tokens, span), jnp.float32),
         ],
         compiler_params=pltpu.CompilerParams(vmem_limit_bytes=32 * 1024 * 1024),
+        cost_estimate=vector_cost(tokens * nstate * channels),
         name="scan_local",
     )(x, dt, w_dt, bias[None], a_log, b_wide, c_wide)
 
@@ -179,6 +409,7 @@
         ],
         scratch_shapes=[pltpu.VMEM((tokens, span), jnp.float32)],
         compiler_params=pltpu.CompilerParams(vmem_limit_bytes=32 * 1024 * 1024),
+        cost_estimate=vector_cost(tokens * nstate * channels),
         name="mix_pack",
     )(x, y, cum, a_log, start, c_wide, skip[None], pack)
 
@@ -257,8 +488,15 @@
     rows = -(-capacity // 16) * 16
     span = 512
     picks = expert_ids[0]
-    up = lax.all_gather(w_up, "seq", axis=1, tiled=True)[0]
-    down = lax.all_gather(w_down, "seq", axis=2, tiled=True)[0]
+    swap = [(i, i ^ 1) for i in range(owners)]
+    up_x = lax.ppermute(w_up[0], "exp", swap)
+    ring = lax.axis_size("seq")
+    up_y = jnp.stack(
+        [
+            lax.ppermute(w_up[0], "seq", [(i, (i + by) % ring) for i in range(ring)])
+            for by in range(2, ring, 2)
+        ]
+    )
     one, two, pack = routing(picks, groups, rows)
     wide = jnp.broadcast_to(b_c[0][:, :, None], b_c.shape[1:] + (LANES,))
     b_wide, c_wide = wide[:, :nstate], wide[:, nstate:]
@@ -276,22 +514,10 @@
     first = jax.nn.sigmoid(gap)
     weights = jnp.concatenate([first, 1.0 - first], axis=1)
 
-    lanes = [[2 * g + h for g in range(groups)] for h in range(2)]
-    swap = [(i, i ^ 1) for i in range(owners)]
-    exchange = functools.partial(
-        lax.all_to_all, axis_name="exp", split_axis=0, concat_axis=0, axis_index_groups=lanes, tiled=True
-    )
-
-    def half(block):
-        hidden = jnp.dot(block, up, preferred_element_type=jnp.float32)
-        hidden = jax.nn.silu(hidden).astype(jnp.bfloat16)
-        return jnp.dot(hidden, down, preferred_element_type=jnp.float32).astype(jnp.bfloat16)
-
-    mine = exchange(packed.reshape(groups, rows, channels)).reshape(-1, channels)
-    other = lax.ppermute(mine, "exp", swap)
-    theirs = lax.ppermute(half(other), "exp", swap)
-    combined = (half(mine).astype(jnp.float32) + theirs.astype(jnp.float32)).astype(jnp.bfloat16)
-    back = exchange(combined.reshape(groups, rows, channels)).reshape(-1, channels)
+    back = run_experts(
+        packed.reshape(groups, rows, channels), w_up[0], up_x, up_y, w_down[0]
+    )
+    back = back.reshape(-1, channels)
     return run_final(mixer, back, one, two, weights, span)[None]
 
 

time: 349 us -> 211 us (0.60)
  waiting for transfers between devices: 191 us -> 22.6 us
  Pallas kernels: 32.1 us -> 160 us
  blocking collectives: 64.5 us -> 0 us
  matrix products: 18.3 us -> 0.59 us
  between operations: 13.7 us -> 0.26 us
  starting transfers between devices: 16.3 us -> 9.77 us
  local copies, waits for them, and re-layouts: 10.4 us -> 14.2 us
    pallas_call x0 -> x1, Pallas kernels: none -> 127 us  [run_experts(): pl.pallas_call(expert_kernel, in_specs=[any_spec] * 5, out_specs=any_spec...]
    ppermute x2, waiting for transfers between devices: 110 us -> 8.8 us  [the longest x1 8.79 us: per_device(): lax.ppermute(w_up[0], 'seq', [(i, (i + by) % ring) for i in range(ring)])]
    all_to_all x1 -> x0, blocking collectives: 64.5 us -> none  [per_device(): exchange(packed.reshape(groups, rows, channels)).reshape(-1, channels)]
    all_to_all x1 -> x0, waiting for transfers between devices: 55 us -> none  [per_device(): exchange(combined.reshape(groups, rows, channels)).reshape(-1, channels)]
    dot_general x4 -> x0, matrix products: 16.5 us -> none  [the longest x2 8.61 us: half(): jnp.dot(hidden, down, preferred_element_type=jnp.float32)]
    ppermute x3, waiting for transfers between devices: 25.1 us -> 13.8 us  [shift(): return lax.ppermute(value, 'seq', [(i, i + by) for i in range(count - by)])]
    unnamed x35 -> x31, local copies, waits for them, and re-layouts: 8.09 us -> 11.8 us
    all_to_all x1 -> x0, starting transfers between devices: 3.65 us -> none  [per_device(): exchange(combined.reshape(groups, rows, channels)).reshape(-1, channels)]
  transfers between devices with their start and end apart: 8 -> 5, of which waited for: 5 -> 3; matrix products, arithmetic and copies ran while one was open for 4% -> 1% of each run, Pallas kernels for 8% -> 6%
where the time goes in v3:
time: 211 us; the launch traced here: 207 us
  Pallas kernels  160 us (76%)
  waiting for transfers between devices  22.6 us (11%)
  local copies, waits for them, and re-layouts  14.2 us (7%)
  starting transfers between devices  9.77 us (5%)
    pallas_call x1, Pallas kernels, run_experts(): pl.pallas_call(expert_kernel, in_specs=[any_spec] * 5, out_specs=any_spec...  127 us
    pallas_call x1, Pallas kernels, run_scan(): pl.pallas_call(scan_kernel, grid=(channels // span,), in_specs=[cols(toke...  16 us
    ppermute x3, waiting for transfers between devices, shift(): return lax.ppermute(value, 'seq', [(i, i + by) for i in range(count - by)])  13.8 us
    unnamed x31, local copies, waits for them, and re-layouts  11.8 us
    pallas_call x1, Pallas kernels, run_mix(): pl.pallas_call(mix_kernel, grid=(channels // span,), in_specs=[cols(token...  11.7 us
    ppermute x1, waiting for transfers between devices, per_device(): lax.ppermute(w_up[0], 'seq', [(i, (i + by) % ring) for i in range(ring)])  8.79 us
    ppermute x3, starting transfers between devices, shift(): return lax.ppermute(value, 'seq', [(i, i + by) for i in range(count - by)])  8.14 us
    pallas_call x1, Pallas kernels, run_final(): pl.pallas_call(final_kernel, grid=(channels // span,), in_specs=[cols(tok...  4.41 us
  transfers between devices with their start and end apart: 5, of which 3 were waited for; matrix products, arithmetic and copies ran while one was open for 1% of the time, Pallas kernels for 6%

profile of v3, /device:TPU:0, one launch (start us, length us, event | category | flops | bytes accessed | tf_op | source)
XLA Modules:
  0.0 207.4 jit_solution(17297618219958308598)
XLA Ops:
  0.0 0.0 copy-start
  0.0 0.0 copy-start.10
  0.0 0.0 copy-start.3
  0.0 0.8 fusion.9
  0.8 0.1 copy.29
  0.9 0.1 copy.28
  1.0 0.0 copy-start.6
  1.0 0.3 broadcast_in_dim.36.c_ref
  1.3 0.3 broadcast_in_dim.35.b_ref
  1.6 0.0 copy-done.10
  1.7 0.0 copy-done.3
  1.7 0.9 copy-done.6
  2.6 0.0 copy-start.7
  2.6 1.2 copy-done.7
  3.8 0.0 copy-start.9
  3.8 0.8 copy-done.9
  4.6 0.0 copy-start.14
  4.6 16.0 %scan_local.1 = (f32[128,4096]{1,0:T(8,128)S(1)}, f32[128,4096]{1,0:T(8,128)S(1)}, f32[16,4096]{1,0:T(8,128)S(1)}) custom-call(bf16[128,4096]{1,0:T(8,128)(2,1)S(1)} %bitcast.23, bf16[128,256]{1,0:T(8,128)(2,1)S(1)} %bitcast.25, bf16[256,4096]{1,0:T(8,128)(2,1)S(1)} %copy-done.6, f32[1,4096]{1,0:T(1,128)S(1)} %bitcast.26, f32[16,4096]{1,0:T(8,128)S(1)} %copy-done.3, ...), custom_call_target="tpu_custom_call" | custom-call | flops 17179869184 | bytes 50331648 | tf_op jit(solution)/shard_map/scan_local/pallas_call | solution.py:360
  20.6 0.0 copy-start.12
  20.7 1.3 copy-done.12
  22.0 0.0 copy-start.11
  22.0 0.0 copy-start.4
  22.0 1.3 copy-done.4
  23.4 2.4 %collective-permute-start = (f32[17,4096]{1,0:T(8,128)S(1)}, f32[17,4096]{1,0:T(8,128)S(1)}, u32[]{:S(2)}, u32[]{:S(2)}) collective-permute-start(f32[17,4096]{1,0:T(8,128)S(1)} %pad_maximum_fusion), channel_id=1, source_target_pairs={{0,8},{8,16},{16,24},{1,9},{9,17},{17,25},{2,10},{10,18},{18,26},{... | collective-permute-start | bytes 835592 | tf_op jit(solution)/shard_map/ppermute | solution.py:440
  25.8 4.4 %collective-permute-start.1 = (f32[17,4096]{1,0:T(8,128)S(1)}, f32[17,4096]{1,0:T(8,128)S(1)}, u32[]{:S(2)}, u32[]{:S(2)}) collective-permute-start(f32[17,4096]{1,0:T(8,128)S(1)} %pad_maximum_fusion), channel_id=1, source_target_pairs={{0,16},{8,24},{1,17},{9,25},{2,18},{10,26},{3,19},{11,27},{4,20},{... | collective-permute-start | bytes 835592 | tf_op jit(solution)/shard_map/ppermute | solution.py:440
  30.2 1.3 collective-permute-start.2
  31.5 0.1 collective-permute-start.4
  31.6 1.6 collective-permute-start.3
  33.2 0.0 copy-done.14
  33.2 0.1 copy.30
  33.3 0.1 eq.101
  33.4 0.2 fusion
  33.6 0.1 convert_element_type.19
  33.8 0.0 copy-start.5
  33.8 0.2 slice_reduce_fusion.3
  34.0 0.2 slice_reduce_fusion.1
  34.2 0.1 fusion.3
  34.3 0.0 collective-permute-done
  34.3 5.4 %collective-permute-done.1 = f32[17,4096]{1,0:T(8,128)S(1)} collective-permute-done((f32[17,4096]{1,0:T(8,128)S(1)}, f32[17,4096]{1,0:T(8,128)S(1)}, u32[]{:S(2)}, u32[]{:S(2)}) %collective-permute-start.1) | collective-permute-done | bytes 278560 | tf_op jit(solution)/shard_map/ppermute | solution.py:440
  39.7 8.4 %collective-permute-done.2 = f32[17,4096]{1,0:T(8,128)S(1)} collective-permute-done((f32[17,4096]{1,0:T(8,128)S(1)}, f32[17,4096]{1,0:T(8,128)S(1)}, u32[]{:S(2)}, u32[]{:S(2)}) %collective-permute-start.2) | collective-permute-done | bytes 278560 | tf_op jit(solution)/shard_map/ppermute | solution.py:440
  48.2 0.2 fusion.1.start_ref
  48.3 0.0 copy-done.11
  48.3 0.0 copy-done.5
  48.3 0.0 copy-start.8
  48.4 1.2 copy-done.8
  49.6 0.0 copy-start.13
  49.6 1.6 copy-done.13
  51.2 11.7 %mix_pack.1 = (bf16[128,4096]{1,0:T(8,128)(2,1)S(1)}, bf16[320,4096]{1,0:T(8,128)(2,1)S(1)}) custom-call(bf16[128,4096]{1,0:T(8,128)(2,1)S(1)} %bitcast.24, f32[128,4096]{1,0:T(8,128)S(1)} %copy-done.13, f32[128,4096]{1,0:T(8,128)S(1)} %copy-done.5, f32[16,4096]{1,0:T(8,128)S(1)} %copy-done.3, f32[16,4096]{1,0:T(8,128)S(1)} %fusion.1.start_ref, ...), custom_call_target="tpu_custom_call" | custom-call | flops 17179869184 | bytes 50331648 | tf_op jit(solution)/shard_map/mix_pack/pallas_call | solution.py:392
  62.9 0.0 copy-start.2
  62.9 1.5 copy-done.2
  64.4 0.0 copy-done
  64.4 0.4 subtract_reduce_fusion
  64.9 0.1 copy.32.w_ref
  65.0 8.8 %collective-permute-done.4 = bf16[1024,640]{1,0:T(8,128)(2,1)} collective-permute-done((bf16[1024,640]{1,0:T(8,128)(2,1)}, bf16[1024,640]{1,0:T(8,128)(2,1)}, u32[]{:S(2)}, u32[]{:S(2)}) %collective-permute-start.4) | collective-permute-done | bytes 1310752 | tf_op jit(solution)/shard_map/ppermute | solution.py:496
  73.8 0.0 collective-permute-done.3.up_x_ref
  73.8 127.5 %experts.1 = bf16[4,80,4096]{2,1,0:T(8,128)(2,1)} custom-call(bf16[4,80,4096]{2,1,0:T(8,128)(2,1)} %bitcast.22, bf16[1024,640]{1,0:T(8,128)(2,1)} %bitcast.9.up_ref, bf16[1024,640]{1,0:T(8,128)(2,1)} %collective-permute-done.3.up_x_ref, bf16[1,1024,640]{2,1,0:T(8,128)(2,1)} %bitcast.10.up_y_ref, bf16[640,1024]{1,0:T(8,128)(2,1)} %bitcast.29), custom_call_target="tpu_custom_call" | custom-call | tf_op jit(solution)/shard_map/experts/pallas_call | solution.py:324
  201.3 0.0 copy-start.1
  201.3 1.7 copy-done.1
  203.0 4.4 %final_sum.1 = bf16[128,4096]{1,0:T(8,128)(2,1)} custom-call(bf16[128,4096]{1,0:T(8,128)(2,1)S(1)} %get-tuple-element.13.mixer_ref, bf16[320,4096]{1,0:T(8,128)(2,1)S(1)} %bitcast.21, bf16[128,320]{1,0:T(8,128)(2,1)S(1)} %get-tuple-element.23.one_ref, bf16[128,320]{1,0:T(8,128)(2,1)S(1)} %get-tuple-element.24.two_ref, f32[128,2]{1,0:T(8,128)S(1)} %copy.32.w_ref), custom_call_target="tpu_custom_call" | custom-call | tf_op jit(solution)/shard_map/final_sum/pallas_call | solution.py:421
  (9 shorter events, 0.1 us)
Async XLA Ops:
  0.0 64.4 %copy-start = (bf16[4,4096]{1,0:T(4,128)(2,1)S(1)}, bf16[4,4096]{1,0:T(4,128)(2,1)}, u32[]{:S(2)}) copy-start(bf16[4,4096]{1,0:T(4,128)(2,1)} %param.18) | copy-start | bytes 98308
  0.0 1.6 copy-start.10
  0.0 1.7 copy-start.3
  1.0 1.6 copy-start.6
  2.6 1.2 copy-start.7
  3.8 0.8 copy-start.9
  4.6 28.5 %copy-start.14 = (s32[1,128,2]{1,2,0:T(2,128)S(1)}, s32[1,128,2]{1,2,0:T(2,128)}, u32[]{:S(2)}) copy-start(s32[1,128,2]{1,2,0:T(2,128)} %param.19) | copy-start | bytes 3076
  20.6 1.3 copy-start.12
  22.0 26.3 %copy-start.11 = (f32[4096]{0:T(1024)S(1)}, f32[4096]{0:T(1024)}, u32[]{:S(2)}) copy-start(f32[4096]{0:T(1024)} %param.17) | copy-start | bytes 49156
  22.0 1.3 copy-start.4
  23.4 11.0 %collective-permute-start = (f32[17,4096]{1,0:T(8,128)S(1)}, f32[17,4096]{1,0:T(8,128)S(1)}, u32[]{:S(2)}, u32[]{:S(2)}) collective-permute-start(f32[17,4096]{1,0:T(8,128)S(1)} %pad_maximum_fusion), channel_id=1, source_target_pairs={{0,8},{8,16},{16,24},{1,9},{9,17},{17,25},{2,10},{10,18},{18,26},{... | collective-permute-start | bytes 835592 | tf_op jit(solution)/shard_map/ppermute | solution.py:440
  25.8 14.0 %collective-permute-start.1 = (f32[17,4096]{1,0:T(8,128)S(1)}, f32[17,4096]{1,0:T(8,128)S(1)}, u32[]{:S(2)}, u32[]{:S(2)}) collective-permute-start(f32[17,4096]{1,0:T(8,128)S(1)} %pad_maximum_fusion), channel_id=1, source_target_pairs={{0,16},{8,24},{1,17},{9,25},{2,18},{10,26},{3,19},{11,27},{4,20},{... | collective-permute-start | bytes 835592 | tf_op jit(solution)/shard_map/ppermute | solution.py:440
  30.2 18.0 %collective-permute-start.2 = (f32[17,4096]{1,0:T(8,128)S(1)}, f32[17,4096]{1,0:T(8,128)S(1)}, u32[]{:S(2)}, u32[]{:S(2)}) collective-permute-start(f32[17,4096]{1,0:T(8,128)S(1)} %pad_maximum_fusion), channel_id=1, source_target_pairs={{0,24},{1,25},{2,26},{3,27},{4,28},{5,29},{6,30},{7,31}} | collective-permute-start | bytes 835592 | tf_op jit(solution)/shard_map/ppermute | solution.py:440
  31.5 42.3 %collective-permute-start.4 = (bf16[1024,640]{1,0:T(8,128)(2,1)}, bf16[1024,640]{1,0:T(8,128)(2,1)}, u32[]{:S(2)}, u32[]{:S(2)}) collective-permute-start(bf16[1024,640]{1,0:T(8,128)(2,1)} %bitcast.9.up_ref), channel_id=1, source_target_pairs={{0,16},{8,24},{16,0},{24,8},{1,17},{9,25},{17,1},{25,9},{2,18},{10... | collective-permute-start | bytes 3932168 | tf_op jit(solution)/shard_map/ppermute | solution.py:496
  31.6 42.2 %collective-permute-start.3 = (bf16[1024,640]{1,0:T(8,128)(2,1)}, bf16[1024,640]{1,0:T(8,128)(2,1)}, u32[]{:S(2)}, u32[]{:S(2)}) collective-permute-start(bf16[1024,640]{1,0:T(8,128)(2,1)} %bitcast.9.up_ref), channel_id=1, source_target_pairs={{0,1},{1,0},{2,3},{3,2},{4,5},{5,4},{6,7},{7,6},{8,9},{9,8},{10,11... | collective-permute-start | bytes 3932168 | tf_op jit(solution)/shard_map/ppermute | solution.py:492
  33.8 14.6 %copy-start.5 = (f32[128,4096]{1,0:T(8,128)S(1)}, f32[128,4096]{1,0:T(8,128)}, u32[]{:S(2)}) copy-start(f32[128,4096]{1,0:T(8,128)} %copy-done.4) | copy-start | bytes 6291460
  48.3 1.2 copy-start.8
  49.6 1.6 copy-start.13
  62.9 1.5 copy-start.2
  201.3 1.7 copy-start.1

commit v4 on v3

--- a/solution.py
+++ b/solution.py
@@ -75,37 +75,39 @@
         end_ref[:, j * LANES : (j + 1) * LANES] = states[j]
 
 
-def mix_kernel(
-    x_ref, y_ref, cum_ref, alog_ref, start_ref, c_ref, skip_ref, pack_ref, mixer_ref, packed_ref, y_s
+def mix_columns(
+    column, span, x_ref, y_ref, cum_ref, alog_ref, start_ref, c_ref, skip_ref, pack_ref, mixer_ref, packed, y_s
 ):
-    tokens, channels = x_ref.shape
-    tiles = channels // LANES
-    rates = [
-        -jnp.exp(alog_ref[:, j * LANES : (j + 1) * LANES]) * LOG2E for j in range(tiles)
-    ]
-    starts = [start_ref[:, j * LANES : (j + 1) * LANES] for j in range(tiles)]
+    tokens = x_ref.shape[0]
+    groups, rows, _ = packed.shape
+    tiles = span // LANES
+    lanes = [pl.ds(pl.multiple_of(column + j * LANES, LANES), LANES) for j in range(tiles)]
+    every = pl.ds(pl.multiple_of(column, span), span)
+    rates = [-jnp.exp(alog_ref[:, at]) * LOG2E for at in lanes]
+    starts = [start_ref[:, at] for at in lanes]
 
     def body(group, carry):
         base = pl.multiple_of(group * 8, 8)
         partial = [[] for _ in range(tiles)]
-        cum8 = cum_ref[pl.ds(base, 8), :]
+        cum8 = cum_ref[pl.ds(base, 8), every]
         for i in range(8):
             ct = c_ref[base + i]
             for j in range(tiles):
-                cols = slice(j * LANES, (j + 1) * LANES)
-                d = cum8[i : i + 1, cols]
+                d = cum8[i : i + 1, j * LANES : (j + 1) * LANES]
                 partial[j].append(fold_states(ct * (jnp.exp2(rates[j] * d) * starts[j])))
         for j in range(tiles):
             y_s[pl.ds(base, 8), j * LANES : (j + 1) * LANES] = fold(partial[j])
         return carry
 
     lax.fori_loop(0, tokens // 8, body, 0)
-    mixer = (y_s[...] + y_ref[...] + skip_ref[...] * x_ref[...].astype(jnp.float32)).astype(
-        jnp.bfloat16
-    )
-    mixer_ref[...] = mixer
-    packed_ref[...] = jnp.dot(pack_ref[...], mixer, preferred_element_type=jnp.float32).astype(
-        jnp.bfloat16
+    mixer = (
+        y_s[...] + y_ref[:, every] + skip_ref[:, every] * x_ref[:, every].astype(jnp.float32)
+    ).astype(jnp.bfloat16)
+    mixer_ref[:, every] = mixer
+    packed[:, :, every] = (
+        jnp.dot(pack_ref[...], mixer, preferred_element_type=jnp.float32)
+        .astype(jnp.bfloat16)
+        .reshape(groups, rows, span)
     )
 
 
@@ -121,12 +123,13 @@
 
 
 def expert_kernel(
-    packed_ref, up_ref, up_x_ref, up_y_ref, down_ref, back_ref,
-    recv, wu, wd, comb,
-    local_sem, own_sem, up_y_sem, z_send, z_recv, r_send, r_recv,
+    x_in, y_in, cum_in, alog_in, start_in, c_in, skip_in, pack_in,
+    up_ref, up_x_ref, down_ref, back_ref, mixer_ref,
+    packed, recv, wu, wd, comb, y_s,
+    local_sem, own_sem, z_send, z_recv, r_send, r_recv,
     x_send, x_recv, y_send, y_recv, c_send, c_recv,
 ):
-    groups, rows, channels = packed_ref.shape
+    groups, rows, channels = packed.shape
     _, shards, depth, hidden_units = wu.shape
     lines = shards // 2
     me, here = lax.axis_index("exp"), lax.axis_index("seq")
@@ -165,86 +168,115 @@
     pl.semaphore_signal(barrier, inc=1, device_id=sibling, device_id_type=mesh_id)
     pl.semaphore_wait(barrier, groups + lines)
 
-    def z_copy(k):
+    def columns(i):
+        return pl.ds(pl.multiple_of(i * depth, depth), depth)
+
+    def z_copy(k, i):
         to = lax.rem(z + k, groups)
         return remote(
-            packed_ref.at[to], recv.at[z], z_send.at[k], z_recv.at[z], {"exp": 2 * to + h}
+            packed.at[to, :, columns(i)],
+            recv.at[z, :, columns(i)],
+            z_send.at[k * shards + i],
+            z_recv.at[z * shards + i],
+            {"exp": 2 * to + h},
         )
 
-    def r_copy(k):
+    def r_copy(k, i):
         src = behind(k)
         return remote(
-            comb.at[src], back_ref.at[z], r_send.at[k], r_recv.at[z], {"exp": 2 * src + h}
+            comb.at[src, :, columns(i)],
+            back_ref.at[z, :, columns(i)],
+            r_send.at[k * shards + i],
+            r_recv.at[z * shards + i],
+            {"exp": 2 * src + h},
         )
 
     def half_of(q):
         return h if q == 0 else 1 - h
 
-    def y_copy(q, j):
-        src = down_ref if q == 0 else wd.at[1 - h, here]
-        return remote(
-            src, wd.at[half_of(q), here], y_send.at[q, j], y_recv.at[q, y], line_peer(j)
-        )
-
-    def x_copy(j):
-        if j == 0:
-            return remote(down_ref, wd.at[h, here], x_send.at[0], x_recv.at[y], partner)
+    cut = hidden_units // 32 * 16
+
+    def y_copy(kind, j):
+        src, dst = (
+            (up_ref, wu.at[h, here]),
+            (down_ref, wd.at[h, here]),
+            (wd.at[1 - h, here, pl.ds(0, cut)], wd.at[1 - h, here, pl.ds(0, cut)]),
+        )[kind]
+        return remote(src, dst, y_send.at[kind, j], y_recv.at[kind, y], line_peer(j))
+
+    def x_copy(kind, j):
         line = line_behind(j)
-        return remote(
-            up_y_ref.at[j - 1], wu.at[h, 2 * line + core], x_send.at[j], x_recv.at[line], partner
-        )
+        shard = 2 * line + core
+        low = wd.at[h, shard, pl.ds(cut, hidden_units - cut)]
+        src, dst = ((down_ref, wd.at[h, here]), (wu.at[h, shard], wu.at[h, shard]), (low, low))[kind]
+        return remote(src, dst, x_send.at[kind, j], x_recv.at[kind, line], partner)
 
     def c_copy(w, q, j):
         line = line_behind(j)
         shard = 2 * line + core
         dst = (wu if w == 0 else wd).at[half_of(q), shard]
-        if j == 0:
-            src = ((up_ref, up_x_ref), (down_ref, dst))[w][q]
-        elif w == 0 and q == 0:
-            src = up_y_ref.at[j - 1]
-        else:
-            src = dst
+        src = ((up_ref, up_x_ref), (down_ref, dst))[w][q] if j == 0 else dst
         at = (2 * w + half_of(q)) * lines + line
         return remote(src, dst, c_send.at[(2 * w + q) * lines + j], c_recv.at[at], sibling)
 
-    for k in range(1, groups):
-        z_copy(k).start()
     for j in range(1, lines):
         y_copy(0, j).start()
-    for j in range(lines):
-        x_copy(j).start()
+    x_copy(0, 0).start()
     local = [
-        pltpu.make_async_copy(packed_ref.at[z], recv.at[z], local_sem.at[0]),
         pltpu.make_async_copy(up_ref, wu.at[h, here], own_sem.at[0]),
         pltpu.make_async_copy(up_x_ref, wu.at[1 - h, here], own_sem.at[1]),
         pltpu.make_async_copy(down_ref, wd.at[h, here], own_sem.at[2]),
     ]
-    for j in range(1, lines):
-        local.append(
-            pltpu.make_async_copy(
-                up_y_ref.at[j - 1], wu.at[h, 2 * line_behind(j) + core], up_y_sem.at[j]
-            )
-        )
     for copy in local:
         copy.start()
     c_copy(0, 0, 0).start()
     c_copy(0, 1, 0).start()
     c_copy(1, 0, 0).start()
-    for j in range(1, lines):
+
+    span = y_s.shape[1]
+
+    def mix_step(i, carry):
+        def inner(n, inner_carry):
+            mix_columns(
+                i * depth + n * span, span, x_in, y_in, cum_in, alog_in, start_in, c_in, skip_in,
+                pack_in, mixer_ref, packed, y_s,
+            )
+            return inner_carry
+
+        lax.fori_loop(0, depth // span, inner, 0)
+        for k in range(1, groups):
+            z_copy(k, i).start()
+        return carry
+
+    lax.fori_loop(0, shards, mix_step, 0)
+
+    for j in range(1, lines):
+        line = line_behind(j)
+        wait_into(wu.at[h, 2 * line + core], y_recv.at[0, line])
+        y_copy(1, j).start()
+        x_copy(1, j).start()
         c_copy(0, 0, j).start()
-    wait_into(wd.at[1 - h, here], x_recv.at[y])
-    for j in range(1, lines):
-        y_copy(1, j).start()
+    wait_into(wd.at[1 - h, here], x_recv.at[0, y])
+    for j in range(1, lines):
+        y_copy(2, j).start()
     c_copy(1, 1, 0).start()
     for j in range(1, lines):
         line = line_behind(j)
-        wait_into(wu.at[1 - h, 2 * line + core], x_recv.at[line])
+        shard = 2 * line + core
+        wait_into(wd.at[h, shard], y_recv.at[1, line])
+        x_copy(2, j).start()
+        c_copy(1, 0, j).start()
+    for j in range(1, lines):
+        line = line_behind(j)
+        shard = 2 * line + core
+        wait_into(wu.at[1 - h, shard], x_recv.at[1, line])
         c_copy(0, 1, j).start()
-    for q in range(2):
-        for j in range(1, lines):
-            line = line_behind(j)
-            wait_into(wd.at[half_of(q), 2 * line + core], y_recv.at[q, line])
-            c_copy(1, q, j).start()
+    for j in range(1, lines):
+        line = line_behind(j)
+        shard = 2 * line + core
+        wait_into(wd.at[1 - h, shard, pl.ds(0, cut)], y_recv.at[2, line])
+        wait_into(wd.at[1 - h, shard, pl.ds(cut, hidden_units - cut)], x_recv.at[2, line])
+        c_copy(1, 1, j).start()
     for copy in local:
         copy.wait()
     for w in range(2):
@@ -258,14 +290,20 @@
 
     def compute(first, second):
         sources = [behind(first), behind(second)]
-        for k, src in zip((first, second), sources):
-            if k:
-                wait_into(recv.at[src], z_recv.at[src])
         zero = jnp.zeros((2 * rows, hidden_units), jnp.float32)
 
         def up_step(i, acc):
-            cols = pl.ds(pl.multiple_of(i * depth, depth), depth)
-            block = jnp.concatenate([recv[src, :, cols] for src in sources], axis=0)
+            cols = columns(i)
+            for k, src in zip((first, second), sources):
+                if k:
+                    wait_into(recv.at[src, :, cols], z_recv.at[src * shards + i])
+            block = jnp.concatenate(
+                [
+                    (recv if k else packed)[src, :, cols]
+                    for k, src in zip((first, second), sources)
+                ],
+                axis=0,
+            )
             return tuple(
                 acc[n] + jnp.dot(block, wu[n, i], preferred_element_type=jnp.float32)
                 for n in range(2)
@@ -275,7 +313,7 @@
         hidden = [(p / (1.0 + jnp.exp(-p))).astype(jnp.bfloat16) for p in pre]
 
         def down_step(i, carry):
-            cols = pl.ds(pl.multiple_of(i * depth, depth), depth)
+            cols = columns(i)
             total = sum(
                 jnp.dot(hidden[n], wd[n, i], preferred_element_type=jnp.float32)
                 .astype(jnp.bfloat16)
@@ -284,13 +322,12 @@
             ).astype(jnp.bfloat16)
             for n, src in enumerate(sources):
                 comb[src, :, cols] = total[n * rows : (n + 1) * rows]
+            for k in (first, second):
+                if k:
+                    r_copy(k, i).start()
             return carry
 
         lax.fori_loop(0, shards, down_step, 0)
-        for k in (first, second):
-            if k:
-                r_copy(k).start()
-
     order = list(range(1, groups)) + [0]
     for k in range(0, groups, 2):
         compute(order[k], order[k + 1])
@@ -299,50 +336,63 @@
     keep.wait()
     for k in range(1, groups):
         src = behind(k)
-        wait_into(back_ref.at[src], r_recv.at[src])
-        z_copy(k).wait_send()
-        r_copy(k).wait_send()
-    for j in range(lines):
-        x_copy(j).wait_send()
-    for j in range(1, lines):
-        for q in range(2):
-            y_copy(q, j).wait_send()
+
+        def finish(i, carry):
+            wait_into(back_ref.at[src, :, columns(i)], r_recv.at[src * shards + i])
+            z_copy(k, i).wait_send()
+            r_copy(k, i).wait_send()
+            return carry
+
+        lax.fori_loop(0, shards, finish, 0)
+    x_copy(0, 0).wait_send()
+    for j in range(1, lines):
+        for kind in range(3):
+            y_copy(kind, j).wait_send()
+        x_copy(1, j).wait_send()
+        x_copy(2, j).wait_send()
     for w in range(2):
         for q in range(2):
             for j in range(lines):
                 c_copy(w, q, j).wait_send()
 
 
-def run_experts(packed, w_up, up_x, up_y, w_down):
-    groups, rows, channels = packed.shape
+def run_experts(mix_inputs, groups, span, w_up, up_x, w_down):
+    tokens, channels = mix_inputs[0].shape
+    rows = mix_inputs[-1].shape[0] // groups
     depth, hidden_units = w_up.shape
     shards = channels // depth
     lines = shards // 2
+    span = min(span, depth)
     dma = pltpu.SemaphoreType.DMA
     any_spec = pl.BlockSpec(memory_space=pl.ANY)
+    vmem_spec = pl.BlockSpec(memory_space=pltpu.VMEM)
     bf16 = jnp.bfloat16
     return pl.pallas_call(
         expert_kernel,
-        in_specs=[any_spec] * 5,
-        out_specs=any_spec,
-        out_shape=jax.ShapeDtypeStruct(packed.shape, bf16),
+        in_specs=[vmem_spec] * len(mix_inputs) + [any_spec] * 3,
+        out_specs=[any_spec, vmem_spec],
+        out_shape=[
+            jax.ShapeDtypeStruct((groups, rows, channels), bf16),
+            jax.ShapeDtypeStruct((tokens, channels), bf16),
+        ],
         scratch_shapes=[
+            pltpu.VMEM((groups, rows, channels), bf16),
             pltpu.VMEM((groups, rows, channels), bf16),
             pltpu.VMEM((2, shards, depth, hidden_units), bf16),
             pltpu.VMEM((2, shards, hidden_units, depth), bf16),
             pltpu.VMEM((groups, rows, channels), bf16),
+            pltpu.VMEM((tokens, span), jnp.float32),
             dma((1,)),
             dma((3,)),
-            dma((lines,)),
         ]
-        + [dma((groups,)) for _ in range(4)]
-        + [dma((lines,)), dma((lines,)), dma((2, lines)), dma((2, lines))]
+        + [dma((groups * shards,)) for _ in range(4)]
+        + [dma((3, lines)) for _ in range(4)]
         + [dma((4 * lines,)), dma((4 * lines,))],
         compiler_params=pltpu.CompilerParams(
-            collective_id=0, has_side_effects=True, vmem_limit_bytes=56 * 1024 * 1024
+            collective_id=0, has_side_effects=True, vmem_limit_bytes=58 * 1024 * 1024
         ),
         name="experts",
-    )(packed, w_up, up_x, up_y, w_down)
+    )(*mix_inputs, w_up, up_x, w_down)
 
 
 def whole_spec(*shape):
@@ -385,35 +435,6 @@
     )(x, dt, w_dt, bias[None], a_log, b_wide, c_wide)
 
 
-def run_mix(x, y, cum, a_log, start, c_wide, skip, pack, span):
-    tokens, channels = x.shape
-    nstate, slots = a_log.shape[0], pack.shape[0]
-    cols = lambda rows: pl.BlockSpec((rows, span), lambda i: (0, i))
-    return pl.pallas_call(
-        mix_kernel,
-        grid=(channels // span,),
-        in_specs=[
-            cols(tokens),
-            cols(tokens),
-            cols(tokens),
-            cols(nstate),
-            cols(nstate),
-            whole_spec(tokens, nstate, LANES),
-            cols(1),
-            whole_spec(slots, tokens),
-        ],
-        out_specs=[cols(tokens), cols(slots)],
-        out_shape=[
-            jax.ShapeDtypeStruct((tokens, channels), jnp.bfloat16),
-            jax.ShapeDtypeStruct((slots, channels), jnp.bfloat16),
-        ],
-        scratch_shapes=[pltpu.VMEM((tokens, span), jnp.float32)],
-        compiler_params=pltpu.CompilerParams(vmem_limit_bytes=32 * 1024 * 1024),
-        cost_estimate=vector_cost(tokens * nstate * channels),
-        name="mix_pack",
-    )(x, y, cum, a_log, start, c_wide, skip[None], pack)
-
-
 def run_final(mixer, back, one, two, weights, span):
     tokens, channels = mixer.shape
     slots = back.shape[0]
@@ -490,20 +511,13 @@
     picks = expert_ids[0]
     swap = [(i, i ^ 1) for i in range(owners)]
     up_x = lax.ppermute(w_up[0], "exp", swap)
-    ring = lax.axis_size("seq")
-    up_y = jnp.stack(
-        [
-            lax.ppermute(w_up[0], "seq", [(i, (i + by) % ring) for i in range(ring)])
-            for by in range(2, ring, 2)
-        ]
-    )
     one, two, pack = routing(picks, groups, rows)
     wide = jnp.broadcast_to(b_c[0][:, :, None], b_c.shape[1:] + (LANES,))
     b_wide, c_wide = wide[:, :nstate], wide[:, nstate:]
     y, cum, end_state = run_scan(x, dt, w_dt, dt_bias, a_log, b_wide, c_wide, span)
     start = carry_in(-jnp.exp(a_log), cum[-1:], end_state)
-    mixer, packed = run_mix(x, y, cum, a_log, start, c_wide, d_skip, pack, span)
-
+    mix_inputs = (x, y, cum, a_log, start, c_wide, d_skip[None], pack)
+    back, mixer = run_experts(mix_inputs, groups, span, w_up[0], up_x, w_down[0])
     logits = jnp.dot(mixer, w_router.T, preferred_element_type=jnp.float32)
     ids = jnp.arange(groups, dtype=jnp.int32)
     gap = jnp.sum(
@@ -514,9 +528,6 @@
     first = jax.nn.sigmoid(gap)
     weights = jnp.concatenate([first, 1.0 - first], axis=1)
 
-    back = run_experts(
-        packed.reshape(groups, rows, channels), w_up[0], up_x, up_y, w_down[0]
-    )
     back = back.reshape(-1, channels)
     return run_final(mixer, back, one, two, weights, span)[None]
 

time: 211 us -> 213 us (level)
  local copies, waits for them, and re-layouts: 14.2 us -> 8.93 us
  other arithmetic: 0.41 us -> 3.7 us
    ppermute x1, waiting for transfers between devices: 0.01 us -> 15.3 us  [per_device(): up_x = lax.ppermute(w_up[0], 'exp', swap)]
    ppermute x1 -> x0, waiting for transfers between devices: 8.79 us -> none  [per_device(): lax.ppermute(w_up[0], 'seq', [(i, (i + by) % ring) for i in range(ring)])]
    ppermute x3, waiting for transfers between devices: 13.8 us -> 8.41 us  [shift(): return lax.ppermute(value, 'seq', [(i, i + by) for i in range(count - by)])]
    unnamed x31 -> x25, local copies, waits for them, and re-layouts: 11.8 us -> 6.55 us
    pallas_call x2 -> x1, Pallas kernels: 139 us -> 141 us  [run_experts(): pl.pallas_call(expert_kernel, in_specs=[vmem_spec] * len(mix_inputs) + [a...]
  transfers between devices with their start and end apart: 5 -> 4, of which waited for: 3 -> 3; matrix products, arithmetic and copies ran while one was open for 1% -> 2% of each run, Pallas kernels for 6% -> 0%
where the time goes in v4:
time: 213 us; the launch traced here: 210 us
  Pallas kernels  161 us (76%)
  waiting for transfers between devices  23.7 us (11%)
  starting transfers between devices  11.1 us (5%)
  local copies, waits for them, and re-layouts  8.93 us (4%)
  other arithmetic  3.7 us (2%)
    pallas_call x1, Pallas kernels, run_experts(): pl.pallas_call(expert_kernel, in_specs=[vmem_spec] * len(mix_inputs) + [a...  141 us
    pallas_call x1, Pallas kernels, run_scan(): pl.pallas_call(scan_kernel, grid=(channels // span,), in_specs=[cols(toke...  16 us
    ppermute x1, waiting for transfers between devices, per_device(): up_x = lax.ppermute(w_up[0], 'exp', swap)  15.3 us
    ppermute x3, starting transfers between devices, shift(): return lax.ppermute(value, 'seq', [(i, i + by) for i in range(count - by)])  9.59 us
    ppermute x3, waiting for transfers between devices, shift(): return lax.ppermute(value, 'seq', [(i, i + by) for i in range(count - by)])  8.41 us
    unnamed x25, local copies, waits for them, and re-layouts  6.55 us
    pallas_call x1, Pallas kernels, run_final(): pl.pallas_call(final_kernel, grid=(channels // span,), in_specs=[cols(tok...  4.39 us
  transfers between devices with their start and end apart: 4, of which 3 were waited for; matrix products, arithmetic and copies ran while one was open for 2% of the time, Pallas kernels for 0%

profile of v4, /device:TPU:0, one launch (start us, length us, event | category | flops | bytes accessed | tf_op | source)
XLA Modules:
  0.0 210.4 jit_solution(14670899846130903733)
XLA Ops:
  0.0 0.0 copy-start
  0.0 0.0 copy-start.9
  0.0 0.0 copy-start.10
  0.0 0.0 copy-start.7
  0.0 0.8 fusion.9
  0.8 0.1 copy.29
  0.9 0.1 copy.28
  1.0 0.0 copy-start.6
  1.0 0.3 broadcast_in_dim.36.c_ref.c_in
  1.3 0.0 copy-start.2
  1.3 0.3 broadcast_in_dim.35.b_ref
  1.7 0.0 copy-done.9
  1.7 0.0 copy-done.10
  1.7 0.0 copy-done.7
  1.7 0.5 copy-done.6
  2.2 0.0 copy-start.8
  2.2 1.6 copy-done.8
  3.8 0.0 copy-start.11
  3.8 16.0 %scan_local.1 = (f32[128,4096]{1,0:T(8,128)S(1)}, f32[128,4096]{1,0:T(8,128)S(1)}, f32[16,4096]{1,0:T(8,128)S(1)}) custom-call(bf16[128,4096]{1,0:T(8,128)(2,1)S(1)} %bitcast.21, bf16[128,256]{1,0:T(8,128)(2,1)S(1)} %bitcast.22, bf16[256,4096]{1,0:T(8,128)(2,1)S(1)} %copy-done.8, f32[1,4096]{1,0:T(1,128)S(1)} %bitcast.23, f32[16,4096]{1,0:T(8,128)S(1)} %copy-done.7, ...), custom_call_target="tpu_custom_call" | custom-call | flops 17179869184 | bytes 50331648 | tf_op jit(solution)/shard_map/scan_local/pallas_call | solution.py:410
  19.8 0.0 copy-done.2
  19.8 0.0 copy-start.5
  19.8 1.3 copy-done.5
  21.2 0.0 copy-start.4
  21.2 2.4 %collective-permute-start = (f32[17,4096]{1,0:T(8,128)S(1)}, f32[17,4096]{1,0:T(8,128)S(1)}, u32[]{:S(2)}, u32[]{:S(2)}) collective-permute-start(f32[17,4096]{1,0:T(8,128)S(1)} %pad_maximum_fusion), channel_id=1, source_target_pairs={{0,8},{8,16},{16,24},{1,9},{9,17},{17,25},{2,10},{10,18},{18,26},{... | collective-permute-start | bytes 835592 | tf_op jit(solution)/shard_map/ppermute | solution.py:461
  23.6 5.2 %collective-permute-start.1 = (f32[17,4096]{1,0:T(8,128)S(1)}, f32[17,4096]{1,0:T(8,128)}, u32[]{:S(2)}, u32[]{:S(2)}) collective-permute-start(f32[17,4096]{1,0:T(8,128)S(1)} %pad_maximum_fusion), channel_id=1, source_target_pairs={{0,16},{8,24},{1,17},{9,25},{2,18},{10,26},{3,19},{11,27},{4,20},{... | collective-permute-start | bytes 835592 | tf_op jit(solution)/shard_map/ppermute | solution.py:461
  28.8 2.0 collective-permute-start.2
  30.8 1.5 collective-permute-start.3
  32.3 0.0 copy-done.11
  32.3 0.1 copy.30
  32.4 0.1 eq.101
  32.6 0.2 fusion
  32.8 0.1 convert_element_type.19
  33.0 0.2 slice_reduce_fusion.3
  33.1 0.7 fusion.6.pack_in
  33.8 0.2 slice_reduce_fusion.1
  34.0 0.1 fusion.3
  34.1 0.0 collective-permute-done
  34.1 3.5 %collective-permute-done.1 = f32[17,4096]{1,0:T(8,128)} collective-permute-done((f32[17,4096]{1,0:T(8,128)S(1)}, f32[17,4096]{1,0:T(8,128)}, u32[]{:S(2)}, u32[]{:S(2)}) %collective-permute-start.1) | collective-permute-done | bytes 278560 | tf_op jit(solution)/shard_map/ppermute | solution.py:461
  37.6 0.9 fusion.8
  38.5 4.9 %collective-permute-done.2 = f32[17,4096]{1,0:T(8,128)} collective-permute-done((f32[17,4096]{1,0:T(8,128)S(1)}, f32[17,4096]{1,0:T(8,128)}, u32[]{:S(2)}, u32[]{:S(2)}) %collective-permute-start.2) | collective-permute-done | bytes 278560 | tf_op jit(solution)/shard_map/ppermute | solution.py:461
  43.5 1.9 fusion.1.start_in
  45.4 15.3 %collective-permute-done.3.up_x_ref = bf16[1024,640]{1,0:T(8,128)(2,1)} collective-permute-done((bf16[1024,640]{1,0:T(8,128)(2,1)}, bf16[1024,640]{1,0:T(8,128)(2,1)}, u32[]{:S(2)}, u32[]{:S(2)}) %collective-permute-start.3) | collective-permute-done | bytes 1310752 | tf_op jit(solution)/shard_map/ppermute | solution.py:513
  60.7 0.0 copy-done.4
  60.7 140.5 %experts.1 = (bf16[4,80,4096]{2,1,0:T(8,128)(2,1)}, bf16[128,4096]{1,0:T(8,128)(2,1)}) custom-call(bf16[128,4096]{1,0:T(8,128)(2,1)} %bitcast.20, f32[128,4096]{1,0:T(8,128)} %copy-done.5, f32[128,4096]{1,0:T(8,128)} %copy-done.4, f32[16,4096]{1,0:T(8,128)} %alog_in.1, f32[16,4096]{1,0:T(8,128)} %fusion.1.start_in, f32[128,16,128]{2,1,0:T(8,128)} %copy-done.2, ...), custom_call_target="tpu_custom_call" | custom-call | tf_op jit(solution)/shard_map/experts/pallas_call | solution.py:370
  201.2 0.0 copy-done
  201.2 1.6 subtract_reduce_fusion
  202.9 0.1 copy.32.w_ref
  203.0 0.0 copy-start.1
  203.0 1.2 copy-done.1
  204.3 0.0 copy-start.3
  204.3 1.7 copy-done.3
  206.0 4.4 %final_sum.1 = bf16[128,4096]{1,0:T(8,128)(2,1)} custom-call(bf16[128,4096]{1,0:T(8,128)(2,1)S(1)} %copy-done.1, bf16[320,4096]{1,0:T(8,128)(2,1)S(1)} %bitcast.19, bf16[128,320]{1,0:T(8,128)(2,1)S(1)} %get-tuple-element.23.one_ref, bf16[128,320]{1,0:T(8,128)(2,1)S(1)} %get-tuple-element.24.two_ref, f32[128,2]{1,0:T(8,128)S(1)} %copy.32.w_ref), custom_call_target="tpu_custom_call" | custom-call | tf_op jit(solution)/shard_map/final_sum/pallas_call | solution.py:442
  (7 shorter events, 0.1 us)
Async XLA Ops:
  0.0 201.2 %copy-start = (bf16[4,4096]{1,0:T(4,128)(2,1)S(1)}, bf16[4,4096]{1,0:T(4,128)(2,1)}, u32[]{:S(2)}) copy-start(bf16[4,4096]{1,0:T(4,128)(2,1)} %param.18) | copy-start | bytes 98308
  0.0 1.7 copy-start.9
  0.0 1.7 copy-start.10
  0.0 1.7 copy-start.7
  1.0 1.2 copy-start.6
  1.3 18.5 %copy-start.2 = (f32[128,16,128]{2,1,0:T(8,128)}, f32[128,16,128]{2,1,0:T(8,128)S(1)}, u32[]{:S(2)}) copy-start(f32[128,16,128]{2,1,0:T(8,128)S(1)} %broadcast_in_dim.36.c_ref.c_in) | copy-start | bytes 3145732
  2.2 1.6 copy-start.8
  3.8 28.5 %copy-start.11 = (s32[1,128,2]{1,2,0:T(2,128)S(1)}, s32[1,128,2]{1,2,0:T(2,128)}, u32[]{:S(2)}) copy-start(s32[1,128,2]{1,2,0:T(2,128)} %param.19) | copy-start | bytes 3076
  19.8 1.3 copy-start.5
  21.2 39.5 %copy-start.4 = (f32[128,4096]{1,0:T(8,128)}, f32[128,4096]{1,0:T(8,128)S(1)}, u32[]{:S(2)}) copy-start(f32[128,4096]{1,0:T(8,128)S(1)} %get-tuple-element.11.cum_in) | copy-start | bytes 6291460
  21.2 12.9 %collective-permute-start = (f32[17,4096]{1,0:T(8,128)S(1)}, f32[17,4096]{1,0:T(8,128)S(1)}, u32[]{:S(2)}, u32[]{:S(2)}) collective-permute-start(f32[17,4096]{1,0:T(8,128)S(1)} %pad_maximum_fusion), channel_id=1, source_target_pairs={{0,8},{8,16},{16,24},{1,9},{9,17},{17,25},{2,10},{10,18},{18,26},{... | collective-permute-start | bytes 835592 | tf_op jit(solution)/shard_map/ppermute | solution.py:461
  23.6 14.0 %collective-permute-start.1 = (f32[17,4096]{1,0:T(8,128)S(1)}, f32[17,4096]{1,0:T(8,128)}, u32[]{:S(2)}, u32[]{:S(2)}) collective-permute-start(f32[17,4096]{1,0:T(8,128)S(1)} %pad_maximum_fusion), channel_id=1, source_target_pairs={{0,16},{8,24},{1,17},{9,25},{2,18},{10,26},{3,19},{11,27},{4,20},{... | collective-permute-start | bytes 835592 | tf_op jit(solution)/shard_map/ppermute | solution.py:461
  28.8 14.7 %collective-permute-start.2 = (f32[17,4096]{1,0:T(8,128)S(1)}, f32[17,4096]{1,0:T(8,128)}, u32[]{:S(2)}, u32[]{:S(2)}) collective-permute-start(f32[17,4096]{1,0:T(8,128)S(1)} %pad_maximum_fusion), channel_id=1, source_target_pairs={{0,24},{1,25},{2,26},{3,27},{4,28},{5,29},{6,30},{7,31}} | collective-permute-start | bytes 835592 | tf_op jit(solution)/shard_map/ppermute | solution.py:461
  30.8 29.9 %collective-permute-start.3 = (bf16[1024,640]{1,0:T(8,128)(2,1)}, bf16[1024,640]{1,0:T(8,128)(2,1)}, u32[]{:S(2)}, u32[]{:S(2)}) collective-permute-start(bf16[1024,640]{1,0:T(8,128)(2,1)} %bitcast.8.up_ref), channel_id=1, source_target_pairs={{0,1},{1,0},{2,3},{3,2},{4,5},{5,4},{6,7},{7,6},{8,9},{9,8},{10,11... | collective-permute-start | bytes 3932168 | tf_op jit(solution)/shard_map/ppermute | solution.py:513
  203.0 1.2 copy-start.1
  204.3 1.7 copy-start.3

commit v5 on v4

--- a/solution.py
+++ b/solution.py
@@ -215,7 +215,7 @@
         line = line_behind(j)
         shard = 2 * line + core
         dst = (wu if w == 0 else wd).at[half_of(q), shard]
-        src = ((up_ref, up_x_ref), (down_ref, dst))[w][q] if j == 0 else dst
+        src = ((up_ref, up_x_ref.at[1 - h]), (down_ref, dst))[w][q] if j == 0 else dst
         at = (2 * w + half_of(q)) * lines + line
         return remote(src, dst, c_send.at[(2 * w + q) * lines + j], c_recv.at[at], sibling)
 
@@ -224,7 +224,7 @@
     x_copy(0, 0).start()
     local = [
         pltpu.make_async_copy(up_ref, wu.at[h, here], own_sem.at[0]),
-        pltpu.make_async_copy(up_x_ref, wu.at[1 - h, here], own_sem.at[1]),
+        pltpu.make_async_copy(up_x_ref.at[1 - h], wu.at[1 - h, here], own_sem.at[1]),
         pltpu.make_async_copy(down_ref, wd.at[h, here], own_sem.at[2]),
     ]
     for copy in local:
@@ -509,8 +509,8 @@
     rows = -(-capacity // 16) * 16
     span = 512
     picks = expert_ids[0]
-    swap = [(i, i ^ 1) for i in range(owners)]
-    up_x = lax.ppermute(w_up[0], "exp", swap)
+    pairs = [[i, i + 1] for i in range(0, owners, 2)]
+    up_x = lax.all_gather(w_up[0], "exp", axis_index_groups=pairs)
     one, two, pack = routing(picks, groups, rows)
     wide = jnp.broadcast_to(b_c[0][:, :, None], b_c.shape[1:] + (LANES,))
     b_wide, c_wide = wide[:, :nstate], wide[:, nstate:]

time: 213 us -> 237 us (1.11)
  between operations: 0.22 us -> 13.6 us
  waiting for transfers between devices: 23.7 us -> 34.8 us
    all_gather x0 -> x1, waiting for transfers between devices: none -> 25 us  [per_device(): up_x = lax.all_gather(w_up[0], 'exp', axis_index_groups=pairs)]
    ppermute x1 -> x0, waiting for transfers between devices: 15.3 us -> none  [per_device(): up_x = lax.ppermute(w_up[0], 'exp', swap)]
where the time goes in v5:
time: 237 us; the launch traced here: 236 us
  Pallas kernels  163 us (69%)
  waiting for transfers between devices  34.8 us (15%)
  between operations  13.6 us (6%)
  starting transfers between devices  9.62 us (4%)
  local copies, waits for them, and re-layouts  8.96 us (4%)
  other arithmetic  3.7 us (2%)
    pallas_call x1, Pallas kernels, run_experts(): pl.pallas_call(expert_kernel, in_specs=[vmem_spec] * len(mix_inputs) + [a...  143 us
    all_gather x1, waiting for transfers between devices, per_device(): up_x = lax.all_gather(w_up[0], 'exp', axis_index_groups=pairs)  25 us
    pallas_call x1, Pallas kernels, run_scan(): pl.pallas_call(scan_kernel, grid=(channels // span,), in_specs=[cols(toke...  16 us
    ppermute x3, waiting for transfers between devices, shift(): return lax.ppermute(value, 'seq', [(i, i + by) for i in range(count - by)])  9.84 us
    ppermute x3, starting transfers between devices, shift(): return lax.ppermute(value, 'seq', [(i, i + by) for i in range(count - by)])  9.59 us
    unnamed x25, local copies, waits for them, and re-layouts  6.56 us
  transfers between devices with their start and end apart: 4, of which 3 were waited for; matrix products, arithmetic and copies ran while one was open for 2% of the time, Pallas kernels for 0%

profile of v5, /device:TPU:0, one launch (start us, length us, event | category | flops | bytes accessed | tf_op | source)
XLA Modules:
  0.0 235.8 jit_solution(15155839819780991697)
XLA Ops:
  6.5 0.0 copy-start
  6.5 0.0 copy-start.9
  6.5 0.0 copy-start.10
  6.5 0.0 copy-start.7
  6.5 0.0 all-gather.2.cloned.1.call-start
  6.6 0.8 fusion.9
  7.4 0.1 copy.29
  7.5 0.1 copy.28
  7.6 0.0 copy-start.6
  7.6 0.3 broadcast_in_dim.36.c_ref.c_in
  7.9 0.0 copy-start.1
  7.9 0.3 broadcast_in_dim.35.b_ref
  8.2 0.0 copy-done.9
  8.2 0.0 copy-done.10
  8.3 0.0 copy-done.7
  8.3 0.5 copy-done.6
  8.8 0.0 copy-start.8
  8.8 1.6 copy-done.8
  10.4 0.0 copy-start.11
  10.4 16.0 %scan_local.1 = (f32[128,4096]{1,0:T(8,128)S(1)}, f32[128,4096]{1,0:T(8,128)S(1)}, f32[16,4096]{1,0:T(8,128)S(1)}) custom-call(bf16[128,4096]{1,0:T(8,128)(2,1)S(1)} %bitcast.21, bf16[128,256]{1,0:T(8,128)(2,1)S(1)} %bitcast.22, bf16[256,4096]{1,0:T(8,128)(2,1)S(1)} %copy-done.8, f32[1,4096]{1,0:T(1,128)S(1)} %bitcast.23, f32[16,4096]{1,0:T(8,128)S(1)} %copy-done.7, ...), custom_call_target="tpu_custom_call" | custom-call | flops 17179869184 | bytes 50331648 | tf_op jit(solution)/shard_map/scan_local/pallas_call | solution.py:410
  26.4 0.0 copy-done.1
  26.4 0.0 copy-start.5
  26.4 1.3 copy-done.5
  27.8 0.0 copy-start.4
  27.8 2.4 %collective-permute-start = (f32[17,4096]{1,0:T(8,128)S(1)}, f32[17,4096]{1,0:T(8,128)S(1)}, u32[]{:S(2)}, u32[]{:S(2)}) collective-permute-start(f32[17,4096]{1,0:T(8,128)S(1)} %pad_maximum_fusion), channel_id=1, source_target_pairs={{0,8},{8,16},{16,24},{1,9},{9,17},{17,25},{2,10},{10,18},{18,26},{... | collective-permute-start | bytes 835592 | tf_op jit(solution)/shard_map/ppermute | solution.py:461
  30.2 5.2 %collective-permute-start.1 = (f32[17,4096]{1,0:T(8,128)S(1)}, f32[17,4096]{1,0:T(8,128)}, u32[]{:S(2)}, u32[]{:S(2)}) collective-permute-start(f32[17,4096]{1,0:T(8,128)S(1)} %pad_maximum_fusion), channel_id=1, source_target_pairs={{0,16},{8,24},{1,17},{9,25},{2,18},{10,26},{3,19},{11,27},{4,20},{... | collective-permute-start | bytes 835592 | tf_op jit(solution)/shard_map/ppermute | solution.py:461
  35.4 2.0 collective-permute-start.2
  37.4 0.0 all-gather.2.cloned.1.call-update
  37.4 0.0 copy-done.11
  37.4 0.1 copy.30
  37.6 0.1 eq.101
  37.7 0.2 fusion
  37.9 0.1 convert_element_type.19
  38.1 0.2 slice_reduce_fusion.3
  38.3 0.7 fusion.6.pack_in
  38.9 0.2 slice_reduce_fusion.1
  39.1 0.1 fusion.3
  39.2 0.0 collective-permute-done
  39.2 4.9 %collective-permute-done.1 = f32[17,4096]{1,0:T(8,128)} collective-permute-done((f32[17,4096]{1,0:T(8,128)S(1)}, f32[17,4096]{1,0:T(8,128)}, u32[]{:S(2)}, u32[]{:S(2)}) %collective-permute-start.1) | collective-permute-done | bytes 278560 | tf_op jit(solution)/shard_map/ppermute | solution.py:461
  44.2 0.9 fusion.8
  45.1 4.9 %collective-permute-done.2 = f32[17,4096]{1,0:T(8,128)} collective-permute-done((f32[17,4096]{1,0:T(8,128)S(1)}, f32[17,4096]{1,0:T(8,128)}, u32[]{:S(2)}, u32[]{:S(2)}) %collective-permute-start.2) | collective-permute-done | bytes 278560 | tf_op jit(solution)/shard_map/ppermute | solution.py:461
  50.0 1.9 fusion.1.start_in
  51.9 0.0 copy-done.4
  51.9 25.0 %all-gather.2.cloned.1.call-done.up_x_ref = bf16[2,1024,640]{2,1,0:T(8,128)(2,1)} async-done(((bf16[1,1024,640]{2,1,0:T(8,128)(2,1)}), bf16[2,1024,640]{2,1,0:T(8,128)(2,1)}) %all-gather.2.cloned.1.call-update) | async-done | bytes 2621456 | tf_op jit(solution)/shard_map/all_gather | solution.py:513
  76.9 142.9 %experts.1 = (bf16[4,80,4096]{2,1,0:T(8,128)(2,1)}, bf16[128,4096]{1,0:T(8,128)(2,1)}) custom-call(bf16[128,4096]{1,0:T(8,128)(2,1)} %bitcast.20, f32[128,4096]{1,0:T(8,128)} %copy-done.5, f32[128,4096]{1,0:T(8,128)} %copy-done.4, f32[16,4096]{1,0:T(8,128)} %alog_in.1, f32[16,4096]{1,0:T(8,128)} %fusion.1.start_in, f32[128,16,128]{2,1,0:T(8,128)} %copy-done.1, ...), custom_call_target="tpu_custom_call" | custom-call | tf_op jit(solution)/shard_map/experts/pallas_call | solution.py:370
  219.8 0.0 copy-done
  219.8 1.6 subtract_reduce_fusion
  221.5 0.1 copy.32.w_ref
  221.6 0.0 copy-start.2
  221.6 1.2 copy-done.2
  222.8 0.0 copy-start.3
  222.8 1.7 copy-done.3
  224.5 4.4 %final_sum.1 = bf16[128,4096]{1,0:T(8,128)(2,1)} custom-call(bf16[128,4096]{1,0:T(8,128)(2,1)S(1)} %copy-done.2, bf16[320,4096]{1,0:T(8,128)(2,1)S(1)} %bitcast.19, bf16[128,320]{1,0:T(8,128)(2,1)S(1)} %get-tuple-element.23.one_ref, bf16[128,320]{1,0:T(8,128)(2,1)S(1)} %get-tuple-element.24.two_ref, f32[128,2]{1,0:T(8,128)S(1)} %copy.32.w_ref), custom_call_target="tpu_custom_call" | custom-call | tf_op jit(solution)/shard_map/final_sum/pallas_call | solution.py:442
  (7 shorter events, 0.1 us)
Async XLA Ops:
  6.5 213.2 %copy-start = (bf16[4,4096]{1,0:T(4,128)(2,1)S(1)}, bf16[4,4096]{1,0:T(4,128)(2,1)}, u32[]{:S(2)}) copy-start(bf16[4,4096]{1,0:T(4,128)(2,1)} %param.18) | copy-start | bytes 98308
  6.5 1.7 copy-start.9
  6.5 1.7 copy-start.10
  6.5 1.7 copy-start.7
  6.5 70.4 %all-gather.2.cloned.1.call-start = ((), (), s32[]{:S(2)}) async-start(), calls=%async_computation | async-start | bytes 3932160 | tf_op jit(solution)/shard_map/all_gather | solution.py:513
  7.6 1.2 copy-start.6
  7.9 18.5 %copy-start.1 = (f32[128,16,128]{2,1,0:T(8,128)}, f32[128,16,128]{2,1,0:T(8,128)S(1)}, u32[]{:S(2)}) copy-start(f32[128,16,128]{2,1,0:T(8,128)S(1)} %broadcast_in_dim.36.c_ref.c_in) | copy-start | bytes 3145732
  8.8 1.6 copy-start.8
  10.4 27.1 %copy-start.11 = (s32[1,128,2]{1,2,0:T(2,128)S(1)}, s32[1,128,2]{1,2,0:T(2,128)}, u32[]{:S(2)}) copy-start(s32[1,128,2]{1,2,0:T(2,128)} %param.19) | copy-start | bytes 3076
  26.4 1.4 copy-start.5
  27.8 24.2 %copy-start.4 = (f32[128,4096]{1,0:T(8,128)}, f32[128,4096]{1,0:T(8,128)S(1)}, u32[]{:S(2)}) copy-start(f32[128,4096]{1,0:T(8,128)S(1)} %get-tuple-element.11.cum_in) | copy-start | bytes 6291460
  27.8 11.4 %collective-permute-start = (f32[17,4096]{1,0:T(8,128)S(1)}, f32[17,4096]{1,0:T(8,128)S(1)}, u32[]{:S(2)}, u32[]{:S(2)}) collective-permute-start(f32[17,4096]{1,0:T(8,128)S(1)} %pad_maximum_fusion), channel_id=1, source_target_pairs={{0,8},{8,16},{16,24},{1,9},{9,17},{17,25},{2,10},{10,18},{18,26},{... | collective-permute-start | bytes 835592 | tf_op jit(solution)/shard_map/ppermute | solution.py:461
  30.2 14.0 %collective-permute-start.1 = (f32[17,4096]{1,0:T(8,128)S(1)}, f32[17,4096]{1,0:T(8,128)}, u32[]{:S(2)}, u32[]{:S(2)}) collective-permute-start(f32[17,4096]{1,0:T(8,128)S(1)} %pad_maximum_fusion), channel_id=1, source_target_pairs={{0,16},{8,24},{1,17},{9,25},{2,18},{10,26},{3,19},{11,27},{4,20},{... | collective-permute-start | bytes 835592 | tf_op jit(solution)/shard_map/ppermute | solution.py:461
  35.4 14.7 %collective-permute-start.2 = (f32[17,4096]{1,0:T(8,128)S(1)}, f32[17,4096]{1,0:T(8,128)}, u32[]{:S(2)}, u32[]{:S(2)}) collective-permute-start(f32[17,4096]{1,0:T(8,128)S(1)} %pad_maximum_fusion), channel_id=1, source_target_pairs={{0,24},{1,25},{2,26},{3,27},{4,28},{5,29},{6,30},{7,31}} | collective-permute-start | bytes 835592 | tf_op jit(solution)/shard_map/ppermute | solution.py:461
  221.6 1.2 copy-start.2
  222.8 1.7 copy-start.3
Sparse Core Ops, SparseCore 0:
  37.6 39.3 all-gather.1
